TPU v7x, 128 devices: a whole 4x4x4 slice. The times are simulated.
128 devices in a mesh: tm: 4 (over y), rest: 32 (over x, z, core).
Axes of the slice: x: 4, y: 4, z: 4, core: 2. Of those that a mesh axis runs over, the one named last changes fastest.
Arguments:
- slab: float32 [1024, 131072], P('tm', 'rest')
- start_basis: float32 [1024, 128], replicated, may hold values from -6 to 6
- time_rank: int32 [1], replicated, may hold values from 64 to 128
Outputs:
- basis: float32 [1024, 128], replicated
- core: float32 [128, 131072], P('tm', 'rest')
- param_gram: float32 [128, 128], replicated
All inputs are finite; a program needn't handle non-finite values.
Results may differ from a plain program's by a relative error of at most 0.0003.
Values sent between devices are 32-bit elements; how exact they have to be, the bound alone decides.
No kernel may reach another device: no remote copies, remote signals or barrier semaphores. Data moves between devices by JAX's collectives and lax.ppermute only.
A program may use at most 128 MiB of HBM per device.

v0:
```python
import jax
import jax.numpy as jnp
from jax import lax
from jax.sharding import PartitionSpec as P

PARAMS = 128
ITERS = 3


def local(slab, start_basis, time_rank):
    hi = lax.Precision.HIGHEST
    rest_count = lax.axis_size("rest")
    time_local = slab.shape[0]
    columns_all = slab.shape[1] * rest_count
    whole = None
    gram = None
    whole = lax.all_to_all(slab, "tm", split_axis=1, concat_axis=0, tiled=True)
    partial_gram = jnp.dot(whole, whole.T, precision=hi, preferred_element_type=jnp.float32)
    gram = lax.psum(partial_gram, ("tm", "rest")) / float(columns_all)
    basis_iter = start_basis
    for step in range(ITERS):
        image = jnp.dot(gram, basis_iter, precision=hi, preferred_element_type=jnp.float32)
        inner = jnp.dot(image.T, image, precision=hi, preferred_element_type=jnp.float32)
        lower = jnp.linalg.cholesky(inner)
        basis_iter = lax.linalg.triangular_solve(lower, image.T, left_side=True, lower=True).T
    rank_all = basis_iter.shape[1]
    keep = (jnp.arange(rank_all, dtype=jnp.int32) < time_rank[0]).astype(jnp.float32)
    basis = basis_iter * keep[None, :]
    my_rows = lax.dynamic_slice_in_dim(basis, lax.axis_index("tm") * time_local, time_local, 0)
    core = lax.psum_scatter(
        jnp.dot(my_rows.T, slab, precision=hi, preferred_element_type=jnp.float32),
        "tm",
        scatter_dimension=0,
        tiled=True,
    )
    folded = core.reshape(-1, PARAMS)
    partial_param = jnp.dot(folded.T, folded, precision=hi, preferred_element_type=jnp.float32)
    space_all = slab.shape[1] // PARAMS * rest_count
    param_gram = lax.psum(partial_param, ("tm", "rest")) / float(rank_all * space_all)
    return (basis, core, param_gram)


def solution(mesh):
    in_specs = (P("tm", "rest"), P(), P())
    out_specs = (P(), P("tm", "rest"), P())
    return jax.shard_map(local, mesh=mesh, in_specs=in_specs, out_specs=out_specs, check_vma=False)
```

profile of v0, /device:TPU:0, one launch (start us, length us, event | category | flops | bytes accessed | tf_op | source)
XLA Modules:
  0.0 519.6 jit_solution(201842549757248623)
XLA Ops:
  7.2 0.0 copy-start
  7.2 0.0 all-reduce.3.cloned.1.call-start
  7.2 5.7 %copy.14 = f32[256,4096]{0,1:T(8,128)} copy(f32[256,4096]{1,0:T(8,128)} %param.6) | data formatting | bytes 8388608 | tf_op args[0]
  12.9 54.8 %all_to_all.19 = f32[256,4,1024]{0,2,1:T(8,128)} all-to-all(f32[256,4,1024]{0,2,1:T(8,128)} %bitcast.57), channel_id=1, replica_groups=mesh['tm'=4,'rest'=32] {'tm'}, dimensions={1} | all-to-all | bytes 8388608 | tf_op jit(solution)/shard_map/all_to_all | solution.py:17
  67.7 5.4 %copy.15 = f32[4,256,1024]{2,1,0:T(8,128)} copy(f32[4,256,1024]{1,2,0:T(8,128)} %bitcast.56) | data formatting | bytes 8388608 | tf_op jit(solution)/shard_map/all_to_all | solution.py:17
  73.1 18.1 %fusion.33 = f32[1024,1024]{1,0:T(8,128)} fusion(f32[1024,1024]{1,0:T(8,128)} %bitcast.58), kind=kOutput, calls=%fused_computation.48 | convolution fusion | flops 12884901888 | bytes 8388608 | tf_op jit(solution)/shard_map/dot_general | solution.py:18
  91.2 0.0 all-reduce.3.cloned.1.call-update
  91.3 0.2 reduce-scatter.2.cloned.1.call-start
  92.1 153.7 %all-reduce.3.cloned.1.call-done = f32[1024,1024]{1,0:T(8,128)} async-done(((f32[1024,1024]{1,0:T(8,128)}), f32[1024,1024]{1,0:T(8,128)}) %all-reduce.3.cloned.1.call-update) | async-done | bytes 4194320 | tf_op jit(solution)/shard_map/psum | solution.py:19
  245.9 0.0 copy-done
  245.9 5.2 %fusion.4 = f32[1024,128]{1,0:T(8,128)S(1)} fusion(f32[1024,128]{1,0:T(8,128)S(1)} %copy-done, f32[1024,1024]{1,0:T(8,128)} %all-reduce.3.cloned.1.call-done), kind=kOutput, calls=%fused_computation.4 | convolution fusion | flops 1611661312 | bytes 5242880 | tf_op jit(solution)/shard_map/dot_general | solution.py:22
  251.1 1.0 fusion.34
  252.1 0.1 copy.16
  252.2 11.7 %cholesky.59 = f32[128,128]{1,0:T(8,128)S(1)} custom-call(f32[128,128]{1,0:T(8,128)S(1)} %fusion.24), custom_call_target="Cholesky" | custom-call | tf_op jit(solution)/shard_map/jit(cholesky)/cholesky | solution.py:24
  264.0 0.6 compare_reduce_fusion.2
  264.6 0.7 fusion.16
  265.3 9.8 %custom-call.7 = f32[1,128,128]{1,2,0:T(8,128)S(1)} custom-call(f32[1,128,128]{2,1,0:T(8,128)S(1)} %fusion.16), custom_call_target="InvertDiagBlocksLowerTriangular" | custom-call | tf_op jit(solution)/shard_map/triangular_solve/custom-call.0 | solution.py:25
  275.1 0.6 fusion.12
  275.7 5.4 %fusion.2 = f32[1024,128]{1,0:T(8,128)S(1)} fusion(f32[128,1024]{1,0:T(8,128)S(1)} %fusion.12, f32[1024,1024]{1,0:T(8,128)} %all-reduce.3.cloned.1.call-done), kind=kOutput, calls=%fused_computation.2 | convolution fusion | flops 1611661312 | bytes 5242880 | tf_op jit(solution)/shard_map/dot_general | solution.py:22
  281.2 1.0 fusion.35
  282.2 0.1 copy.17
  282.3 11.7 %cholesky.70 = f32[128,128]{1,0:T(8,128)S(1)} custom-call(f32[128,128]{1,0:T(8,128)S(1)} %fusion.22), custom_call_target="Cholesky" | custom-call | tf_op jit(solution)/shard_map/jit(cholesky)/cholesky | solution.py:24
  294.1 0.6 compare_reduce_fusion.1
  294.7 0.7 fusion.17
  295.4 9.8 %custom-call.8 = f32[1,128,128]{1,2,0:T(8,128)S(1)} custom-call(f32[1,128,128]{2,1,0:T(8,128)S(1)} %fusion.17), custom_call_target="InvertDiagBlocksLowerTriangular" | custom-call | tf_op jit(solution)/shard_map/triangular_solve/custom-call.0 | solution.py:25
  305.2 0.6 fusion.10
  305.8 5.5 %fusion = f32[1024,128]{1,0:T(8,128)S(1)} fusion(f32[128,1024]{1,0:T(8,128)S(1)} %fusion.10, f32[1024,1024]{1,0:T(8,128)} %all-reduce.3.cloned.1.call-done), kind=kOutput, calls=%fused_computation | convolution fusion | flops 1611661312 | bytes 5242880 | tf_op jit(solution)/shard_map/dot_general | solution.py:22
  311.3 1.0 fusion.36
  312.3 0.1 copy.18
  312.4 11.7 %cholesky.81 = f32[128,128]{1,0:T(8,128)S(1)} custom-call(f32[128,128]{1,0:T(8,128)S(1)} %fusion.20), custom_call_target="Cholesky" | custom-call | tf_op jit(solution)/shard_map/jit(cholesky)/cholesky | solution.py:24
  324.2 0.6 compare_reduce_fusion
  324.8 0.7 fusion.18
  325.5 9.8 %custom-call.9 = f32[1,128,128]{1,2,0:T(8,128)S(1)} custom-call(f32[1,128,128]{2,1,0:T(8,128)S(1)} %fusion.18), custom_call_target="InvertDiagBlocksLowerTriangular" | custom-call | tf_op jit(solution)/shard_map/triangular_solve/custom-call.0 | solution.py:25
  335.3 0.6 convolution_multiply_fusion
  336.0 5.8 %fusion.14 = f32[128,4096]{1,0:T(8,128)} fusion(f32[256,4096]{1,0:T(8,128)} %param.6, f32[128,1024]{1,0:T(8,128)S(1)} %convolution_multiply_fusion, s32[]{:T(128)S(6)} %select_n.6), kind=kOutput, calls=%fused_computation.15 | convolution fusion | flops 1610612736 | bytes 6422532 | tf_op jit(solution)/shard_map/dot_general | solution.py:31
  341.8 0.0 reduce-scatter.2.cloned.1.call-update
  341.8 0.0 all-reduce.5.cloned.1.call-start
  341.9 28.1 %reduce-scatter.2.cloned.1.call-done = f32[32,4096]{1,0:T(8,128)} async-done(((f32[128,4096]{1,0:T(8,128)}), f32[32,4096]{1,0:T(8,128)}) %reduce-scatter.2.cloned.1.call-update) | async-done | bytes 524304 | tf_op jit(solution)/shard_map/reduce_scatter | solution.py:30
  370.0 1.1 reshape.28
  371.1 1.6 fusion.37
  372.8 0.0 all-reduce.5.cloned.1.call-update
  372.8 1.0 copy.19
  373.8 137.4 %all-reduce.5.cloned.1.call-done = f32[128,128]{1,0:T(8,128)} async-done(((f32[128,128]{1,0:T(8,128)}), f32[128,128]{1,0:T(8,128)}) %all-reduce.5.cloned.1.call-update) | async-done | bytes 65552 | tf_op jit(solution)/shard_map/psum | solution.py:39
  511.2 1.5 broadcast_multiply_fusion
  (7 shorter events, 0.1 us)
Async XLA Ops:
  7.2 238.7 %copy-start = (f32[1024,128]{1,0:T(8,128)S(1)}, f32[1024,128]{1,0:T(8,128)}, u32[]{:S(2)}) copy-start(f32[1024,128]{1,0:T(8,128)} %param.7) | copy-start | bytes 1572868
  7.2 238.7 %all-reduce.3.cloned.1.call-start = ((), (), s32[]{:S(2)}) async-start(), calls=%async_computation.2 | async-start | bytes 8388608 | tf_op jit(solution)/shard_map/psum | solution.py:19
  91.3 278.8 %reduce-scatter.2.cloned.1.call-start = ((), (), s32[]{:S(2)}) async-start(), calls=%async_computation.3 | async-start | bytes 2621440 | tf_op jit(solution)/shard_map/reduce_scatter | solution.py:30
  341.8 169.4 %all-reduce.5.cloned.1.call-start = ((), (), s32[]{:S(2)}) async-start(), calls=%async_computation.4 | async-start | bytes 131072 | tf_op jit(solution)/shard_map/psum | solution.py:39
Sparse Core Ops, SparseCore 0:
  91.4 154.4 all-reduce.2
  341.9 28.0 reduce-scatter.1
  376.0 135.0 all-reduce.4
where the time goes:
time: 529 us; the launch traced here: 520 us
  waiting for transfers between devices  319 us (60%)
  other arithmetic  70.1 us (13%)
  blocking collectives  54.8 us (10%)
  matrix products  46.7 us (9%)
  between operations  15 us (3%)
  local copies, waits for them, and re-layouts  13.5 us (3%)
    psum x1, waiting for transfers between devices, local(): gram = lax.psum(partial_gram, ('tm', 'rest')) / float(columns_all)  154 us
    psum x1, waiting for transfers between devices, local(): lax.psum(partial_param, ('tm', 'rest')) / float(rank_all * space_all)  137 us
    all_to_all x1, blocking collectives, local(): whole = lax.all_to_all(slab, 'tm', split_axis=1, concat_axis=0, tiled=True)  54.8 us
    another operation x9, other arithmetic, local(): lower = jnp.linalg.cholesky(inner)  37.2 us
    another operation x6, other arithmetic, local(): lax.linalg.triangular_solve(lower, image.T, left_side=True, lower=True)  31.4 us
    reduce_scatter x1, waiting for transfers between devices, local(): lax.psum_scatter(jnp.dot(my_rows.T, slab, precision=hi, preferred_element...  28.1 us
    dot_general x1, matrix products, local(): jnp.dot(whole, whole.T, precision=hi, preferred_element_type=jnp.float32)  18.1 us
    dot_general x3, matrix products, local(): jnp.dot(gram, basis_iter, precision=hi, preferred_element_type=jnp.float32)  16.1 us
  transfers between devices with their start and end apart: 3, of which 3 were waited for; matrix products, arithmetic and copies ran while one was open for 0% of the time, Pallas kernels for 0%

commit v1 on v0

v1 whole, which is shorter than its diff:
```python
import jax
import jax.numpy as jnp
from jax import lax
from jax.experimental import pallas as pl
from jax.experimental.pallas import tpu as pltpu
from jax.sharding import PartitionSpec as P

F32, BF16 = jnp.float32, jnp.bfloat16
PARAMS = 128
ITERS = 3
NY, NX, NZ = 4, 4, 4
PAIRS = [(i, j) for i in range(NY) for j in range(i, NY)]
HALF = len(PAIRS) // 2
VMEM, SMEM = pltpu.VMEM, pltpu.SMEM


def rest_index(x, z, c):
    return (x * NZ + z) * 2 + c


def along_y(v, k):
    return lax.ppermute(v, "tm", [(i, (i + k) % NY) for i in range(NY)])


def along_core(v):
    return lax.ppermute(v, "rest", [(i, i ^ 1) for i in range(2 * NX * NZ)])


def along_xz(v, k, first):
    perm = []
    for x in range(NX):
        for z in range(NZ):
            for c in range(2):
                if (c == 0) == first:
                    to = rest_index((x + k) % NX, z, c)
                else:
                    to = rest_index(x, (z + k) % NZ, c)
                perm.append((rest_index(x, z, c), to))
    return lax.ppermute(v, "rest", perm)


def split2(v):
    hi = v.astype(BF16)
    return hi, (v - hi.astype(F32)).astype(BF16)


def split3(v):
    hi = v.astype(BF16)
    rest = v - hi.astype(F32)
    mid = rest.astype(BF16)
    return hi, mid, (rest - mid.astype(F32)).astype(BF16)


def dot(a, b, ca, cb):
    return lax.dot_general(a, b, (((ca,), (cb,)), ((), ())), preferred_element_type=F32)


def gram_kernel(table, w0, w1, w2, w3, send, keep, hi_out, lo_out, hi, lo, sem):
    for k, w in enumerate((w0, w1, w2, w3)):
        h, l = split2(w[...])
        hi[table[k]] = h
        lo[table[k]] = l
    copies = [
        pltpu.make_async_copy(hi, hi_out, sem.at[0]),
        pltpu.make_async_copy(lo, lo_out, sem.at[1]),
    ]
    for copy in copies:
        copy.start()
    for n in range(2 * HALF):
        i, j = table[NY + 2 * n], table[NY + 2 * n + 1]
        out = send if n < HALF else keep
        out[n % HALF] = dot(hi[i], hi[j], 1, 1) + (
            (dot(hi[i], lo[j], 1, 1) + dot(lo[i], hi[j], 1, 1)) + dot(lo[i], lo[j], 1, 1)
        )
    for copy in copies:
        copy.wait()


def partial_gram(table, parts):
    rows, cols = parts[0].shape
    blocks = jax.ShapeDtypeStruct((HALF, rows, rows), F32)
    halves = jax.ShapeDtypeStruct((NY, rows, cols), BF16)
    return pl.pallas_call(
        gram_kernel,
        out_shape=(blocks, blocks, halves, halves),
        in_specs=[pl.BlockSpec(memory_space=SMEM)] + [pl.BlockSpec(memory_space=VMEM)] * 4,
        out_specs=[pl.BlockSpec(memory_space=VMEM)] * 2 + [pl.BlockSpec(memory_space=pl.ANY)] * 2,
        scratch_shapes=[VMEM((NY, rows, cols), BF16)] * 2 + [pltpu.SemaphoreType.DMA((2,))],
        compiler_params=pltpu.CompilerParams(vmem_limit_bytes=40 * 2**20),
        cost_estimate=pl.CostEstimate(flops=2 * 40 * rows * rows * cols, bytes_accessed=11 * 2**20, transcendentals=0),
        name="partial_gram",
    )(table, *parts)


def row_of(v, k):
    return jnp.broadcast_to(v[k : k + 1, :], v.shape)


def cholesky_inverse(work):
    n = work.shape[0]
    r = lax.broadcasted_iota(jnp.int32, (n, n), 0)
    c = lax.broadcasted_iota(jnp.int32, (n, n), 1)
    work[:, n:] = (r == c).astype(F32)
    row = lax.broadcasted_iota(jnp.int32, (8, n), 0)
    panels = []
    for p in range(n // 8):
        left, right = work[8 * p : 8 * p + 8, :n], work[8 * p : 8 * p + 8, n:]
        column = [jnp.broadcast_to(left[:, 8 * p + j : 8 * p + j + 1], (8, n)) for j in range(8)]
        scale = jnp.zeros((8, n), F32)
        for k in range(8):
            pivot = row_of(column[k], k)
            factor = jnp.where(row > k, column[k] * (1.0 / pivot), 0.0)
            scale = jnp.where(row == k, lax.rsqrt(pivot), scale)
            for j in range(k + 1, 8):
                column[j] = column[j] - factor * row_of(column[j], k)
            if k < 7:
                left = left - factor * row_of(left, k)
                right = right - factor * row_of(right, k)
        left, right = left * scale, right * scale
        panels.append(right)
        if p < n // 8 - 1:
            h, m, l = split3(jnp.concatenate([left, right], 1))
            lh, lm, ll = h[:, :n], m[:, :n], l[:, :n]
            work[...] = work[...] - dot(
                jnp.concatenate([lh, lh, lm, lm, lh, ll], 0), jnp.concatenate([h, m, h, m, l, h], 0), 0, 0
            )
    return jnp.concatenate(panels, 0)


def solve_kernel(
    place, rank, *refs, scale
):
    pieces, (start, hi_in, lo_in) = refs[:8], refs[8:11]
    basis_out, core0, core1, core2, core3, param_out = refs[11:17]
    packed, gh, gm, gl, hi, lo, work, core, sem = refs[17:]
    copies = [
        pltpu.make_async_copy(hi_in, hi, sem.at[0]),
        pltpu.make_async_copy(lo_in, lo, sem.at[1]),
    ]
    for copy in copies:
        copy.start()
    rows = pieces[0].shape[1]
    for n, piece in enumerate(pieces):
        for j in range(NX):
            at = pl.multiple_of(place[NY + NX * n + j] * rows, 8)
            packed[pl.ds(at, rows), :] = piece[j]
    t = packed.shape[1]
    for n, (i, j) in enumerate(PAIRS):
        block = packed[n * t : (n + 1) * t, :] * scale
        for k, g in enumerate(split3(block)):
            (gh, gm, gl)[k][i * t : (i + 1) * t, j * t : (j + 1) * t] = g
        if i < j:
            for k, g in enumerate(split3(block.T)):
                (gh, gm, gl)[k][j * t : (j + 1) * t, i * t : (i + 1) * t] = g

    q = start[...].T
    n = q.shape[0]
    for _ in range(ITERS):
        h, m, l = split3(q)
        by_h = dot(jnp.concatenate([h, m, l], 0), gh[...], 1, 0)
        by_m = dot(jnp.concatenate([h, m], 0), gm[...], 1, 0)
        by_l = dot(h, gl[...], 1, 0)
        image = by_h[:n] + ((by_h[n : 2 * n] + by_m[:n]) + (by_h[2 * n :] + by_m[n:] + by_l))
        h, m, l = split3(image)
        by_h = dot(jnp.concatenate([h, m, l], 0), h, 1, 1)
        small = by_h[n : 2 * n] + by_h[2 * n :]
        work[:, :n] = by_h[:n] + ((small + small.T) + dot(m, m, 1, 1))
        ih, im, il = split3(cholesky_inverse(work))
        by_h = dot(jnp.concatenate([ih, im, il], 0), h, 1, 0)
        by_m = dot(jnp.concatenate([ih, im], 0), m, 1, 0)
        q = by_h[:n] + ((by_h[n : 2 * n] + by_m[:n]) + (by_h[2 * n :] + by_m[n:] + dot(ih, l, 1, 0)))

    slot = lax.broadcasted_iota(jnp.int32, q.shape, 0)
    q = jnp.where(slot < rank[0], q, 0.0)
    basis_out[...] = q.T
    for copy in copies:
        copy.wait()
    h, l = split2(q)
    total = None
    for i in range(NY):
        hs, ls = h[:, i * t : (i + 1) * t], l[:, i * t : (i + 1) * t]
        by_hi = dot(jnp.concatenate([hs, ls], 0), hi[i], 1, 0)
        term = by_hi[:n] + (by_hi[n:] + dot(hs, lo[i], 1, 0))
        total = term if total is None else total + term
    core[...] = total
    own = n // NY
    for k, out in enumerate((core0, core1, core2, core3)):
        out[...] = core[pl.ds(pl.multiple_of(place[k] * own, 8), own), :]
    h, l = split2(total)
    param = jnp.zeros((PARAMS, PARAMS), F32)
    for s in range(total.shape[1] // PARAMS):
        hs, ls = h[:, s * PARAMS : (s + 1) * PARAMS], l[:, s * PARAMS : (s + 1) * PARAMS]
        cross = dot(hs, ls, 0, 0)
        param = param + (dot(hs, hs, 0, 0) + (cross + cross.T) + dot(ls, ls, 0, 0))
    param_out[...] = param


def solve(place, rank, pieces, start_basis, hi, lo, scale):
    time_all, ranks = start_basis.shape
    t, width = hi.shape[1:]
    struct = jax.ShapeDtypeStruct
    part = struct((ranks // NY, width), F32)
    vmem = pl.BlockSpec(memory_space=VMEM)
    smem = pl.BlockSpec(memory_space=SMEM)
    anywhere = pl.BlockSpec(memory_space=pl.ANY)

    def body(*refs):
        solve_kernel(*refs, scale=scale)

    return pl.pallas_call(
        body,
        out_shape=(struct((time_all, ranks), F32), part, part, part, part, struct((PARAMS, PARAMS), F32)),
        in_specs=[smem, smem] + [vmem] * 9 + [anywhere] * 2,
        out_specs=[vmem] * 6,
        scratch_shapes=[
            VMEM((len(PAIRS) * t, t), F32),
            VMEM((time_all, time_all), BF16),
            VMEM((time_all, time_all), BF16),
            VMEM((time_all, time_all), BF16),
            VMEM(hi.shape, BF16),
            VMEM(lo.shape, BF16),
            VMEM((ranks, 2 * ranks), F32),
            VMEM((ranks, width), F32),
            pltpu.SemaphoreType.DMA((2,)),
        ],
        compiler_params=pltpu.CompilerParams(vmem_limit_bytes=48 * 2**20),
        cost_estimate=pl.CostEstimate(flops=8 * 10**9, bytes_accessed=9 * 2**20, transcendentals=0),
        name="solve",
    )(place, rank, *pieces, start_basis, hi, lo)


def join_kernel(place, p0, p1, p2, p3, out):
    width = p0.shape[1]
    for k, piece in enumerate((p0, p1, p2, p3)):
        out[:, pl.ds(pl.multiple_of(place[k] * width, 128), width)] = piece[...]


def join_columns(place, pieces):
    rows, width = pieces[0].shape
    return pl.pallas_call(
        join_kernel,
        out_shape=jax.ShapeDtypeStruct((rows, NY * width), F32),
        in_specs=[pl.BlockSpec(memory_space=SMEM)] + [pl.BlockSpec(memory_space=VMEM)] * 4,
        out_specs=pl.BlockSpec(memory_space=VMEM),
        name="join_columns",
    )(place, *pieces)


def take(v, i):
    return lax.dynamic_index_in_dim(v, i, 0, keepdims=False)


def scatter_sum(v, me, move):
    got = [move(take(v, (me + k) % NX), k) for k in (1, 3, 2)]
    return take(v, me) + got[0] + got[1] + got[2]


def exchange_sum(v, move):
    got = [move(v, k) for k in (1, 3, 2)]
    return v + got[0] + got[1] + got[2]


def gather(v, move):
    got = {k: move(v, k) for k in (1, 3, 2)}
    return [v, got[1], got[2], got[3]]


def local(slab, start_basis, time_rank):
    rest_count = lax.axis_size("rest")
    time_local, columns_local = slab.shape
    columns_all = columns_local * rest_count
    width = columns_local // NY
    ranks = start_basis.shape[1]
    me_y = lax.axis_index("tm")
    rest = lax.axis_index("rest")
    core_id, me_z, me_x = rest % 2, (rest // 2) % NZ, rest // (2 * NZ)
    first_me = jnp.where(core_id == 0, me_x, me_z)
    second_me = jnp.where(core_id == 0, me_z, me_x)
    four = jnp.arange(NY, dtype=jnp.int32)

    def columns(k):
        return lax.dynamic_slice_in_dim(slab, (me_y + k) % NY * width, width, 1)

    got = {k: along_y(columns(k), k) for k in (1, 3, 2)}
    parts = [columns(0), got[1], got[2], got[3]]
    source_y = (me_y - four) % NY
    pairs = jnp.array(PAIRS, jnp.int32).reshape(2, HALF * 2)
    table = jnp.concatenate([source_y, take(pairs, 1 - core_id), take(pairs, core_id)])
    send, keep, hi, lo = partial_gram(table, parts)

    rows = HALF * time_local // (NX * NZ)
    v = (keep + along_core(send)).reshape(NX, NZ, rows, time_local)
    v = scatter_sum(v, first_me, lambda u, k: along_xz(u, k, True))
    v = scatter_sum(v, second_me, lambda u, k: along_xz(u, k, False))
    v = exchange_sum(v, along_y)
    v = jnp.stack(gather(v, lambda u, k: along_xz(u, k, False)))
    pieces = gather(v, lambda u, k: along_xz(u, k, True))
    pieces = pieces + [along_core(piece) for piece in pieces]

    def chunk(core, first, second):
        k, j = four[:, None], four[None, :]
        return ((core * NX + (first - k) % NX) * NZ + (second - j) % NZ).reshape(-1)

    place = jnp.concatenate(
        [(me_y + four) % NY, chunk(core_id, first_me, second_me), chunk(1 - core_id, second_me, first_me)]
    )
    basis, *cores, param = solve(place, time_rank, pieces, start_basis, hi, lo, 1.0 / columns_all)

    param = param + along_core(param)
    param = exchange_sum(param, lambda u, k: along_xz(u, k, True))
    param = exchange_sum(param, lambda u, k: along_xz(u, k, False))
    param = exchange_sum(param, along_y)
    space_all = columns_local // PARAMS * rest_count
    param_gram = param / float(ranks * space_all)

    mine = {k: along_y(cores[k], k) for k in (1, 3, 2)}
    core = join_columns(source_y, [cores[0], mine[1], mine[2], mine[3]])
    return (basis, core, param_gram)


def solution(mesh):
    in_specs = (P("tm", "rest"), P(), P())
    out_specs = (P(), P("tm", "rest"), P())
    return jax.shard_map(local, mesh=mesh, in_specs=in_specs, out_specs=out_specs, check_vma=False)
```

time: 529 us -> 191 us (0.36); the launches traced: 520 us -> 191 us
  waiting for transfers between devices: 319 us -> 90.4 us
  other arithmetic: 70.1 us -> 3.64 us
  blocking collectives: 54.8 us -> 0 us
  matrix products: 46.7 us -> 0 us
  starting transfers between devices: 0.29 us -> 42.1 us
  Pallas kernels: 0 us -> 40.3 us
  between operations: 15 us -> 1.53 us
    psum x2 -> x0, waiting for transfers between devices: 291 us -> none  [the longest x1 154 us: local(): gram = lax.psum(partial_gram, ('tm', 'rest')) / float(columns_all)]
    ppermute x0 -> x36, waiting for transfers between devices: none -> 90.4 us  [the longest x12 52.5 us: along_y(): return lax.ppermute(v, 'tm', [(i, (i + k) % NY) for i in range(NY)])]
    another operation x15 -> x1, other arithmetic: 68.6 us -> 0.02 us  [local(): v = jnp.stack(gather(v, lambda u, k: along_xz(u, k, False)))]
    all_to_all x1 -> x0, blocking collectives: 54.8 us -> none  [local(): whole = lax.all_to_all(slab, 'tm', split_axis=1, concat_axis=0, tiled=True)]
    dot_general x9 -> x0, matrix products: 44.7 us -> none  [the longest x1 18.1 us: local(): jnp.dot(whole, whole.T, precision=hi, preferred_element_type=jnp.float32)]
    ppermute x0 -> x36, starting transfers between devices: none -> 42.1 us  [the longest x18 27.1 us: along_xz(): return lax.ppermute(v, 'rest', perm)]
    pallas_call x0 -> x3, Pallas kernels: none -> 40.3 us  [the longest x1 29.5 us: solve(): pl.pallas_call(body, out_shape=(struct((time_all, ranks), F32), part, par...]
    reduce_scatter x1 -> x0, waiting for transfers between devices: 28.1 us -> none  [local(): lax.psum_scatter(jnp.dot(my_rows.T, slab, precision=hi, preferred_element...]
  transfers between devices with their start and end apart: 3 -> 36, of which waited for: 3 -> 29; matrix products, arithmetic and copies ran while one was open for 0% -> 0% of each run, Pallas kernels for 0% -> 1%
where the time goes in v1:
time: 191 us
  waiting for transfers between devices  90.4 us (47%)
  starting transfers between devices  42.1 us (22%)
  Pallas kernels  40.3 us (21%)
  local copies, waits for them, and re-layouts  13.2 us (7%)
  other arithmetic  3.64 us (2%)
    ppermute x12, waiting for transfers between devices, along_y(): return lax.ppermute(v, 'tm', [(i, (i + k) % NY) for i in range(NY)])  52.5 us
    ppermute x18, waiting for transfers between devices, along_xz(): return lax.ppermute(v, 'rest', perm)  32.9 us
    pallas_call x1, Pallas kernels, solve(): pl.pallas_call(body, out_shape=(struct((time_all, ranks), F32), part, par...  29.5 us
    ppermute x18, starting transfers between devices, along_xz(): return lax.ppermute(v, 'rest', perm)  27.1 us
    ppermute x12, starting transfers between devices, along_y(): return lax.ppermute(v, 'tm', [(i, (i + k) % NY) for i in range(NY)])  14.3 us
    unnamed x26, local copies, waits for them, and re-layouts  8.89 us
    pallas_call x1, Pallas kernels, partial_gram(): pl.pallas_call(gram_kernel, out_shape=(blocks, blocks, halves, halves), i...  8.81 us
    ppermute x6, waiting for transfers between devices, along_core(): return lax.ppermute(v, 'rest', [(i, i ^ 1) for i in range(2 * NX * NZ)])  4.96 us
  transfers between devices with their start and end apart: 36, of which 29 were waited for; matrix products, arithmetic and copies ran while one was open for 0% of the time, Pallas kernels for 1%

profile of v1, /device:TPU:0, one launch (start us, length us, event | category | flops | bytes accessed | tf_op | source)
XLA Modules:
  0.0 191.0 jit_solution(389625609995730925)
XLA Ops:
  0.7 4.0 %constant_dynamic-slice_fusion = (f32[256,1024]{1,0:T(8,128)}, f32[256,1024]{1,0:T(8,128)}, f32[256,1024]{1,0:T(8,128)S(1)}, f32[256,1024]{1,0:T(8,128)}) fusion(f32[256,4096]{1,0:T(8,128)} %param.4, s32[]{:T(128)S(6)} %select_n.174, s32[]{:T(128)S(6)} %select_n.170, s32[]{:T(128)S(6)} %select_n.168, s32[]{:T(128)S(6)} %select_n.172), kind=kLoop, calls=%fused_computation.17 | loop fusion | bytes 8388624 | tf_op jit(solution)/shard_map/dynamic_slice | solution.py:282
  4.7 1.7 collective-permute-start
  6.3 2.9 %collective-permute-start.1 = (f32[256,1024]{1,0:T(8,128)}, f32[256,1024]{1,0:T(8,128)S(1)}, u32[]{:S(2)}, u32[]{:S(2)}) collective-permute-start(f32[256,1024]{1,0:T(8,128)} %get-tuple-element.26), channel_id=1, source_target_pairs={{0,64},{32,96},{64,0},{96,32},{1,65},{33,97},{65,1},{97,33},{2,66}... | collective-permute-start | bytes 3145736 | tf_op jit(solution)/shard_map/ppermute | solution.py:22
  9.2 1.3 collective-permute-start.2
  10.7 20.4 %collective-permute-done.w1 = f32[256,1024]{1,0:T(8,128)S(1)} collective-permute-done((f32[256,1024]{1,0:T(8,128)}, f32[256,1024]{1,0:T(8,128)S(1)}, u32[]{:S(2)}, u32[]{:S(2)}) %collective-permute-start) | collective-permute-done | bytes 1048608 | tf_op jit(solution)/shard_map/ppermute | solution.py:22
  31.1 23.6 %collective-permute-done.1.w2 = f32[256,1024]{1,0:T(8,128)S(1)} collective-permute-done((f32[256,1024]{1,0:T(8,128)}, f32[256,1024]{1,0:T(8,128)S(1)}, u32[]{:S(2)}, u32[]{:S(2)}) %collective-permute-start.1) | collective-permute-done | bytes 1048608 | tf_op jit(solution)/shard_map/ppermute | solution.py:22
  54.8 1.0 copy-done.1
  55.8 1.2 copy-done.2
  57.0 8.8 %partial_gram.1 = (f32[5,256,256]{2,1,0:T(8,128)}, f32[5,256,256]{2,1,0:T(8,128)S(1)}, bf16[4,256,1024]{2,1,0:T(8,128)(2,1)S(1)}, bf16[4,256,1024]{2,1,0:T(8,128)(2,1)S(1)}) custom-call(s32[24]{0:T(128)S(1)} %pad_add_fusion.1.table, f32[256,1024]{1,0:T(8,128)S(1)} %get-tuple-element.25.w0, f32[256,1024]{1,0:T(8,128)S(1)} %collective-permute-done.w1, ...), custom_call_target="tpu_custom_call" | custom-call | flops 5368709120 | bytes 11534336 | tf_op jit(solution)/shard_map/partial_gram/pallas_call | solution.py:83
  65.8 1.3 copy-done.4
  67.2 1.4 copy-done.6
  68.5 3.2 %collective-permute-done.3 = f32[5,256,256]{2,1,0:T(8,128)S(1)} collective-permute-done((f32[5,256,256]{2,1,0:T(8,128)}, f32[5,256,256]{2,1,0:T(8,128)S(1)}, u32[]{:S(2)}, u32[]{:S(2)}) %collective-permute-start.3) | collective-permute-done | bytes 1310752 | tf_op jit(solution)/shard_map/ppermute | solution.py:26
  71.8 1.1 copy-done.7
  72.9 1.5 add.313
  74.4 3.1 %collective-permute-start.6 = (f32[4,80,256]{2,1,0:T(8,128)S(1)}, f32[4,80,256]{2,1,0:T(8,128)S(1)}, u32[]{:S(2)}, u32[]{:S(2)}) collective-permute-start(f32[4,80,256]{2,1,0:T(8,128)S(1)} %get-tuple-element.28), channel_id=1, source_target_pairs={{0,16},{1,5},{2,18},{3,7},{4,20},{5,1},{6,22},{7,3},{8,24},{9,13},... | collective-permute-start | bytes 983048 | tf_op jit(solution)/shard_map/ppermute | solution.py:39
  77.5 1.1 collective-permute-start.5
  78.7 0.9 collective-permute-start.4
  79.6 3.5 %collective-permute-done.6 = f32[4,80,256]{2,1,0:T(8,128)S(1)} collective-permute-done((f32[4,80,256]{2,1,0:T(8,128)S(1)}, f32[4,80,256]{2,1,0:T(8,128)S(1)}, u32[]{:S(2)}, u32[]{:S(2)}) %collective-permute-start.6) | collective-permute-done | bytes 327712 | tf_op jit(solution)/shard_map/ppermute | solution.py:39
  83.1 3.6 %collective-permute-done.5 = f32[4,80,256]{2,1,0:T(8,128)S(1)} collective-permute-done((f32[4,80,256]{2,1,0:T(8,128)S(1)}, f32[4,80,256]{2,1,0:T(8,128)S(1)}, u32[]{:S(2)}, u32[]{:S(2)}) %collective-permute-start.5) | collective-permute-done | bytes 327712 | tf_op jit(solution)/shard_map/ppermute | solution.py:39
  87.1 1.1 fusion.1
  88.2 4.0 %collective-permute-start.9 = (f32[80,256]{1,0:T(8,128)S(1)}, f32[80,256]{1,0:T(8,128)S(1)}, u32[]{:S(2)}, u32[]{:S(2)}) collective-permute-start(f32[80,256]{1,0:T(8,128)S(1)} %get-tuple-element.31), channel_id=1, source_target_pairs={{0,4},{1,17},{2,6},{3,19},{4,0},{5,21},{6,2},{7,23},{8,12},{9,25},... | collective-permute-start | bytes 245768 | tf_op jit(solution)/shard_map/ppermute | solution.py:39
  92.1 0.7 collective-permute-start.8
  92.9 1.3 collective-permute-start.7
  94.6 2.0 %collective-permute-done.8 = f32[80,256]{1,0:T(8,128)S(1)} collective-permute-done((f32[80,256]{1,0:T(8,128)S(1)}, f32[80,256]{1,0:T(8,128)S(1)}, u32[]{:S(2)}, u32[]{:S(2)}) %collective-permute-start.8) | collective-permute-done | bytes 81952 | tf_op jit(solution)/shard_map/ppermute | solution.py:39
  96.6 1.9 %collective-permute-done.7 = f32[80,256]{1,0:T(8,128)S(1)} collective-permute-done((f32[80,256]{1,0:T(8,128)S(1)}, f32[80,256]{1,0:T(8,128)S(1)}, u32[]{:S(2)}, u32[]{:S(2)}) %collective-permute-start.7) | collective-permute-done | bytes 81952 | tf_op jit(solution)/shard_map/ppermute | solution.py:39
  98.5 1.8 collective-permute-start.12
  100.3 1.2 collective-permute-start.11
  101.6 0.8 collective-permute-start.10
  102.4 2.2 %collective-permute-done.12 = f32[80,256]{1,0:T(8,128)S(1)} collective-permute-done((f32[80,256]{1,0:T(8,128)S(1)}, f32[80,256]{1,0:T(8,128)S(1)}, u32[]{:S(2)}, u32[]{:S(2)}) %collective-permute-start.12) | collective-permute-done | bytes 81952 | tf_op jit(solution)/shard_map/ppermute | solution.py:22
  104.8 2.5 %collective-permute-done.10 = f32[80,256]{1,0:T(8,128)S(1)} collective-permute-done((f32[80,256]{1,0:T(8,128)S(1)}, f32[80,256]{1,0:T(8,128)S(1)}, u32[]{:S(2)}, u32[]{:S(2)}) %collective-permute-start.10) | collective-permute-done | bytes 81952 | tf_op jit(solution)/shard_map/ppermute | solution.py:22
  107.2 0.7 collective-permute-start.15
  107.9 1.5 collective-permute-start.14
  109.9 1.8 collective-permute-done.15
  111.7 2.1 %collective-permute-done.14 = f32[80,256]{1,0:T(8,128)S(1)} collective-permute-done((f32[80,256]{1,0:T(8,128)S(1)}, f32[80,256]{1,0:T(8,128)S(1)}, u32[]{:S(2)}, u32[]{:S(2)}) %collective-permute-start.14) | collective-permute-done | bytes 81952 | tf_op jit(solution)/shard_map/ppermute | solution.py:39
  113.9 1.9 %collective-permute-done.13 = f32[80,256]{1,0:T(8,128)S(1)} collective-permute-done((f32[80,256]{1,0:T(8,128)S(1)}, f32[80,256]{1,0:T(8,128)S(1)}, u32[]{:S(2)}, u32[]{:S(2)}) %collective-permute-start.13) | collective-permute-done | bytes 81952 | tf_op jit(solution)/shard_map/ppermute | solution.py:39
  115.8 1.5 collective-permute-start.16
  117.4 2.6 %collective-permute-start.17 = (f32[4,80,256]{2,1,0:T(8,128)S(1)}, f32[4,80,256]{2,1,0:T(8,128)S(1)}, u32[]{:S(2)}, u32[]{:S(2)}) collective-permute-start(f32[4,80,256]{2,1,0:T(8,128)S(1)} %pad_maximum_fusion.refs_2_), channel_id=1, source_target_pairs={{0,16},{1,5},{2,18},{3,7},{4,20},{5,1},{6,22},{7,3},{8,24},{9,13},... | collective-permute-start | bytes 983048 | tf_op jit(solution)/shard_map/ppermute | solution.py:39
  119.9 1.5 collective-permute-start.18
  121.6 2.6 %collective-permute-done.16.refs_3_ = f32[4,80,256]{2,1,0:T(8,128)S(1)} collective-permute-done((f32[4,80,256]{2,1,0:T(8,128)S(1)}, f32[4,80,256]{2,1,0:T(8,128)S(1)}, u32[]{:S(2)}, u32[]{:S(2)}) %collective-permute-start.16) | collective-permute-done | bytes 327712 | tf_op jit(solution)/shard_map/ppermute | solution.py:39
  124.2 4.3 %collective-permute-done.17.refs_4_ = f32[4,80,256]{2,1,0:T(8,128)S(1)} collective-permute-done((f32[4,80,256]{2,1,0:T(8,128)S(1)}, f32[4,80,256]{2,1,0:T(8,128)S(1)}, u32[]{:S(2)}, u32[]{:S(2)}) %collective-permute-start.17) | collective-permute-done | bytes 327712 | tf_op jit(solution)/shard_map/ppermute | solution.py:39
  130.6 1.6 copy-done.5
  132.2 29.5 %solve.1 = (f32[1024,128]{1,0:T(8,128)}, f32[32,1024]{1,0:T(8,128)S(1)}, f32[32,1024]{1,0:T(8,128)S(1)}, f32[32,1024]{1,0:T(8,128)S(1)}, f32[32,1024]{1,0:T(8,128)S(1)}, /*index=5*/f32[128,128]{1,0:T(8,128)S(1)}) custom-call(s32[36]{0:T(128)S(1)} %pad_add_fusion.refs_0_, s32[1]{0:T(128)S(6)} %copy.7.refs_1_, f32[4,80,256]{2,1,0:T(8,128)S(1)} %pad_maximum_fusion.refs_2_, ...), custom_call_target="tpu_custom_call" | custom-call | flops 8000000000 | bytes 9437184 | tf_op jit(solution)/shard_map/solve/pallas_call | solution.py:210
  161.7 0.7 copy-done
  162.5 1.1 collective-permute-done.26
  163.6 2.7 %collective-permute-start.29 = (f32[128,128]{1,0:T(8,128)S(1)}, f32[128,128]{1,0:T(8,128)S(1)}, u32[]{:S(2)}, u32[]{:S(2)}) collective-permute-start(f32[128,128]{1,0:T(8,128)S(1)} %add.343), channel_id=1, source_target_pairs={{0,16},{1,5},{2,18},{3,7},{4,20},{5,1},{6,22},{7,3},{8,24},{9,13},... | collective-permute-start | bytes 196616 | tf_op jit(solution)/shard_map/ppermute | solution.py:39
  166.3 1.7 collective-permute-start.28
  168.3 1.2 collective-permute-done.29
  169.5 1.1 collective-permute-done.28
  170.5 2.9 %collective-permute-done.27 = f32[128,128]{1,0:T(8,128)S(1)} collective-permute-done((f32[128,128]{1,0:T(8,128)S(1)}, f32[128,128]{1,0:T(8,128)S(1)}, u32[]{:S(2)}, u32[]{:S(2)}) %collective-permute-start.27) | collective-permute-done | bytes 65568 | tf_op jit(solution)/shard_map/ppermute | solution.py:39
  173.5 1.1 collective-permute-start.32
  174.6 1.3 collective-permute-start.31
  175.9 0.7 collective-permute-start.30
  176.6 1.3 collective-permute-start.24
  177.9 1.5 collective-permute-done.32
  179.4 0.5 collective-permute-start.25
  179.8 1.5 collective-permute-done.30
  181.3 1.5 collective-permute-start.35
  182.9 1.3 collective-permute-start.34
  184.2 0.7 collective-permute-done.23.p1
  184.9 1.2 collective-permute-done.25.p3
  186.1 0.6 copy-done.10
  186.7 1.9 %join_columns.1 = f32[32,4096]{1,0:T(8,128)} custom-call(s32[4]{0:T(128)} %copy-done.11, f32[32,1024]{1,0:T(8,128)} %copy-done, f32[32,1024]{1,0:T(8,128)} %copy-done.8, f32[32,1024]{1,0:T(8,128)} %copy-done.9, f32[32,1024]{1,0:T(8,128)} %copy-done.10), custom_call_target="tpu_custom_call" | custom-call | tf_op jit(solution)/shard_map/join_columns/pallas_call | solution.py:240
  188.6 1.7 collective-permute-done.33
  190.3 0.6 add_multiply_fusion
  (61 shorter events, 3.7 us)
Async XLA Ops:
  0.7 9.9 %copy-start.12 = (s32[2,10]{1,0:T(2,128)S(1)}, s32[2,10]{1,0:T(2,128)}, u32[]{:S(2)}) copy-start(s32[2,10]{1,0:T(2,128)} %constant.173) | copy-start | bytes 244
  4.7 26.5 %collective-permute-start = (f32[256,1024]{1,0:T(8,128)}, f32[256,1024]{1,0:T(8,128)S(1)}, u32[]{:S(2)}, u32[]{:S(2)}) collective-permute-start(f32[256,1024]{1,0:T(8,128)} %get-tuple-element.24), channel_id=1, source_target_pairs={{0,32},{32,64},{64,96},{96,0},{1,33},{33,65},{65,97},{97,1},{2,34}... | collective-permute-start | bytes 3145736 | tf_op jit(solution)/shard_map/ppermute | solution.py:22
  6.3 48.5 %collective-permute-start.1 = (f32[256,1024]{1,0:T(8,128)}, f32[256,1024]{1,0:T(8,128)S(1)}, u32[]{:S(2)}, u32[]{:S(2)}) collective-permute-start(f32[256,1024]{1,0:T(8,128)} %get-tuple-element.26), channel_id=1, source_target_pairs={{0,64},{32,96},{64,0},{96,32},{1,65},{33,97},{65,1},{97,33},{2,66}... | collective-permute-start | bytes 3145736 | tf_op jit(solution)/shard_map/ppermute | solution.py:22
  9.2 46.5 %collective-permute-start.2 = (f32[256,1024]{1,0:T(8,128)}, f32[256,1024]{1,0:T(8,128)}, u32[]{:S(2)}, u32[]{:S(2)}) collective-permute-start(f32[256,1024]{1,0:T(8,128)} %get-tuple-element.23), channel_id=1, source_target_pairs={{0,96},{32,0},{64,32},{96,64},{1,97},{33,1},{65,33},{97,65},{2,98}... | collective-permute-start | bytes 3145736 | tf_op jit(solution)/shard_map/ppermute | solution.py:22
  10.6 55.2 %copy-start.11 = (s32[4]{0:T(128)}, s32[4]{0:T(128)S(1)}, u32[]{:S(2)}) copy-start(s32[4]{0:T(128)S(1)} %and_select_fusion.place) | copy-start | bytes 52
  54.8 1.0 copy-start.1
  55.8 1.2 copy-start.2
  65.8 1.3 copy-start.4
  67.2 1.4 copy-start.6
  68.5 3.2 %collective-permute-start.3 = (f32[5,256,256]{2,1,0:T(8,128)}, f32[5,256,256]{2,1,0:T(8,128)S(1)}, u32[]{:S(2)}, u32[]{:S(2)}) collective-permute-start(f32[5,256,256]{2,1,0:T(8,128)} %get-tuple-element.14), channel_id=1, source_target_pairs={{0,1},{1,0},{2,3},{3,2},{4,5},{5,4},{6,7},{7,6},{8,9},{9,8},{10,11... | collective-permute-start | bytes 3932168 | tf_op jit(solution)/shard_map/ppermute | solution.py:26
  71.8 1.1 copy-start.7
  74.4 8.7 %collective-permute-start.6 = (f32[4,80,256]{2,1,0:T(8,128)S(1)}, f32[4,80,256]{2,1,0:T(8,128)S(1)}, u32[]{:S(2)}, u32[]{:S(2)}) collective-permute-start(f32[4,80,256]{2,1,0:T(8,128)S(1)} %get-tuple-element.28), channel_id=1, source_target_pairs={{0,16},{1,5},{2,18},{3,7},{4,20},{5,1},{6,22},{7,3},{8,24},{9,13},... | collective-permute-start | bytes 983048 | tf_op jit(solution)/shard_map/ppermute | solution.py:39
  77.5 9.2 %collective-permute-start.5 = (f32[4,80,256]{2,1,0:T(8,128)S(1)}, f32[4,80,256]{2,1,0:T(8,128)S(1)}, u32[]{:S(2)}, u32[]{:S(2)}) collective-permute-start(f32[4,80,256]{2,1,0:T(8,128)S(1)} %get-tuple-element.29), channel_id=1, source_target_pairs={{0,24},{1,7},{2,26},{3,1},{4,28},{5,3},{6,30},{7,5},{8,0},{9,15},{... | collective-permute-start | bytes 983048 | tf_op jit(solution)/shard_map/ppermute | solution.py:39
  78.7 8.4 %collective-permute-start.4 = (f32[4,80,256]{2,1,0:T(8,128)S(1)}, f32[4,80,256]{2,1,0:T(8,128)}, u32[]{:S(2)}, u32[]{:S(2)}) collective-permute-start(f32[4,80,256]{2,1,0:T(8,128)S(1)} %get-tuple-element.27), channel_id=1, source_target_pairs={{0,8},{1,3},{2,10},{3,5},{4,12},{5,7},{6,14},{7,1},{8,16},{9,11},{... | collective-permute-start | bytes 983048 | tf_op jit(solution)/shard_map/ppermute | solution.py:39
  88.1 42.4 %copy-start.3 = (f32[1024,128]{1,0:T(8,128)S(1)}, f32[1024,128]{1,0:T(8,128)}, u32[]{:S(2)}) copy-start(f32[1024,128]{1,0:T(8,128)} %refs_10_.1) | copy-start | bytes 1572868
  88.2 6.4 %collective-permute-start.9 = (f32[80,256]{1,0:T(8,128)S(1)}, f32[80,256]{1,0:T(8,128)S(1)}, u32[]{:S(2)}, u32[]{:S(2)}) collective-permute-start(f32[80,256]{1,0:T(8,128)S(1)} %get-tuple-element.31), channel_id=1, source_target_pairs={{0,4},{1,17},{2,6},{3,19},{4,0},{5,21},{6,2},{7,23},{8,12},{9,25},... | collective-permute-start | bytes 245768 | tf_op jit(solution)/shard_map/ppermute | solution.py:39
  92.1 4.4 %collective-permute-start.8 = (f32[80,256]{1,0:T(8,128)S(1)}, f32[80,256]{1,0:T(8,128)S(1)}, u32[]{:S(2)}, u32[]{:S(2)}) collective-permute-start(f32[80,256]{1,0:T(8,128)S(1)} %get-tuple-element.32), channel_id=1, source_target_pairs={{0,6},{1,25},{2,0},{3,27},{4,2},{5,29},{6,4},{7,31},{8,14},{9,1},{... | collective-permute-start | bytes 245768 | tf_op jit(solution)/shard_map/ppermute | solution.py:39
  92.9 5.7 %collective-permute-start.7 = (f32[80,256]{1,0:T(8,128)S(1)}, f32[80,256]{1,0:T(8,128)S(1)}, u32[]{:S(2)}, u32[]{:S(2)}) collective-permute-start(f32[80,256]{1,0:T(8,128)S(1)} %get-tuple-element.30), channel_id=1, source_target_pairs={{0,2},{1,9},{2,4},{3,11},{4,6},{5,13},{6,0},{7,15},{8,10},{9,17},{... | collective-permute-start | bytes 245768 | tf_op jit(solution)/shard_map/ppermute | solution.py:39
  98.5 6.0 %collective-permute-start.12 = (f32[80,256]{1,0:T(8,128)S(1)}, f32[80,256]{1,0:T(8,128)S(1)}, u32[]{:S(2)}, u32[]{:S(2)}) collective-permute-start(f32[80,256]{1,0:T(8,128)S(1)} %fusion.3), channel_id=1, source_target_pairs={{0,64},{32,96},{64,0},{96,32},{1,65},{33,97},{65,1},{97,33},{2,66}... | collective-permute-start | bytes 245768 | tf_op jit(solution)/shard_map/ppermute | solution.py:22
  100.3 4.4 %collective-permute-start.11 = (f32[80,256]{1,0:T(8,128)S(1)}, f32[80,256]{1,0:T(8,128)S(1)}, u32[]{:S(2)}, u32[]{:S(2)}) collective-permute-start(f32[80,256]{1,0:T(8,128)S(1)} %fusion.3), channel_id=1, source_target_pairs={{0,96},{32,0},{64,32},{96,64},{1,97},{33,1},{65,33},{97,65},{2,98}... | collective-permute-start | bytes 245768 | tf_op jit(solution)/shard_map/ppermute | solution.py:22
  101.6 5.7 %collective-permute-start.10 = (f32[80,256]{1,0:T(8,128)S(1)}, f32[80,256]{1,0:T(8,128)S(1)}, u32[]{:S(2)}, u32[]{:S(2)}) collective-permute-start(f32[80,256]{1,0:T(8,128)S(1)} %fusion.3), channel_id=1, source_target_pairs={{0,32},{32,64},{64,96},{96,0},{1,33},{33,65},{65,97},{97,1},{2,34}... | collective-permute-start | bytes 245768 | tf_op jit(solution)/shard_map/ppermute | solution.py:22
  107.2 4.5 %collective-permute-start.15 = (f32[80,256]{1,0:T(8,128)S(1)}, f32[80,256]{1,0:T(8,128)S(1)}, u32[]{:S(2)}, u32[]{:S(2)}) collective-permute-start(f32[80,256]{1,0:T(8,128)S(1)} %add_add_fusion), channel_id=1, source_target_pairs={{0,6},{1,25},{2,0},{3,27},{4,2},{5,29},{6,4},{7,31},{8,14},{9,1},{... | collective-permute-start | bytes 245768 | tf_op jit(solution)/shard_map/ppermute | solution.py:39
  107.9 5.9 %collective-permute-start.14 = (f32[80,256]{1,0:T(8,128)S(1)}, f32[80,256]{1,0:T(8,128)S(1)}, u32[]{:S(2)}, u32[]{:S(2)}) collective-permute-start(f32[80,256]{1,0:T(8,128)S(1)} %add_add_fusion), channel_id=1, source_target_pairs={{0,4},{1,17},{2,6},{3,19},{4,0},{5,21},{6,2},{7,23},{8,12},{9,25},... | collective-permute-start | bytes 245768 | tf_op jit(solution)/shard_map/ppermute | solution.py:39
  109.5 6.3 %collective-permute-start.13 = (f32[80,256]{1,0:T(8,128)S(1)}, f32[80,256]{1,0:T(8,128)S(1)}, u32[]{:S(2)}, u32[]{:S(2)}) collective-permute-start(f32[80,256]{1,0:T(8,128)S(1)} %add_add_fusion), channel_id=1, source_target_pairs={{0,2},{1,9},{2,4},{3,11},{4,6},{5,13},{6,0},{7,15},{8,10},{9,17},{... | collective-permute-start | bytes 245768 | tf_op jit(solution)/shard_map/ppermute | solution.py:39
  115.8 8.4 %collective-permute-start.16 = (f32[4,80,256]{2,1,0:T(8,128)S(1)}, f32[4,80,256]{2,1,0:T(8,128)S(1)}, u32[]{:S(2)}, u32[]{:S(2)}) collective-permute-start(f32[4,80,256]{2,1,0:T(8,128)S(1)} %pad_maximum_fusion.refs_2_), channel_id=1, source_target_pairs={{0,8},{1,3},{2,10},{3,5},{4,12},{5,7},{6,14},{7,1},{8,16},{9,11},{... | collective-permute-start | bytes 983048 | tf_op jit(solution)/shard_map/ppermute | solution.py:39
  117.4 11.1 %collective-permute-start.17 = (f32[4,80,256]{2,1,0:T(8,128)S(1)}, f32[4,80,256]{2,1,0:T(8,128)S(1)}, u32[]{:S(2)}, u32[]{:S(2)}) collective-permute-start(f32[4,80,256]{2,1,0:T(8,128)S(1)} %pad_maximum_fusion.refs_2_), channel_id=1, source_target_pairs={{0,16},{1,5},{2,18},{3,7},{4,20},{5,1},{6,22},{7,3},{8,24},{9,13},... | collective-permute-start | bytes 983048 | tf_op jit(solution)/shard_map/ppermute | solution.py:39
  119.9 8.6 %collective-permute-start.18 = (f32[4,80,256]{2,1,0:T(8,128)S(1)}, f32[4,80,256]{2,1,0:T(8,128)S(1)}, u32[]{:S(2)}, u32[]{:S(2)}) collective-permute-start(f32[4,80,256]{2,1,0:T(8,128)S(1)} %pad_maximum_fusion.refs_2_), channel_id=1, source_target_pairs={{0,24},{1,7},{2,26},{3,1},{4,28},{5,3},{6,30},{7,5},{8,0},{9,15},{... | collective-permute-start | bytes 983048 | tf_op jit(solution)/shard_map/ppermute | solution.py:39
  121.5 8.4 %collective-permute-start.19 = (f32[4,80,256]{2,1,0:T(8,128)S(1)}, f32[4,80,256]{2,1,0:T(8,128)S(1)}, u32[]{:S(2)}, u32[]{:S(2)}) collective-permute-start(f32[4,80,256]{2,1,0:T(8,128)S(1)} %pad_maximum_fusion.refs_2_), channel_id=1, source_target_pairs={{0,1},{1,0},{2,3},{3,2},{4,5},{5,4},{6,7},{7,6},{8,9},{9,8},{10,11... | collective-permute-start | bytes 983048 | tf_op jit(solution)/shard_map/ppermute | solution.py:26
  124.2 5.8 %collective-permute-start.20 = (f32[4,80,256]{2,1,0:T(8,128)S(1)}, f32[4,80,256]{2,1,0:T(8,128)S(1)}, u32[]{:S(2)}, u32[]{:S(2)}) collective-permute-start(f32[4,80,256]{2,1,0:T(8,128)S(1)} %collective-permute-done.16.refs_3_), channel_id=1, source_target_pairs={{0,1},{1,0},{2,3},{3,2},{4,5},{5,4},{6,7},{7,6},{8,9},{9,8},{10,11... | collective-permute-start | bytes 983048 | tf_op jit(solution)/shard_map/ppermute | solution.py:26
  128.5 1.6 collective-permute-start.21
  128.6 2.0 %collective-permute-start.22 = (f32[4,80,256]{2,1,0:T(8,128)S(1)}, f32[4,80,256]{2,1,0:T(8,128)S(1)}, u32[]{:S(2)}, u32[]{:S(2)}) collective-permute-start(f32[4,80,256]{2,1,0:T(8,128)S(1)} %collective-permute-done.18.refs_5_), channel_id=1, source_target_pairs={{0,1},{1,0},{2,3},{3,2},{4,5},{5,4},{6,7},{7,6},{8,9},{9,8},{10,11... | collective-permute-start | bytes 983048 | tf_op jit(solution)/shard_map/ppermute | solution.py:26
  130.6 1.6 copy-start.5
  161.7 0.7 copy-start
  162.4 1.3 collective-permute-start.26
  163.6 5.8 %collective-permute-start.29 = (f32[128,128]{1,0:T(8,128)S(1)}, f32[128,128]{1,0:T(8,128)S(1)}, u32[]{:S(2)}, u32[]{:S(2)}) collective-permute-start(f32[128,128]{1,0:T(8,128)S(1)} %add.343), channel_id=1, source_target_pairs={{0,16},{1,5},{2,18},{3,7},{4,20},{5,1},{6,22},{7,3},{8,24},{9,13},... | collective-permute-start | bytes 196616 | tf_op jit(solution)/shard_map/ppermute | solution.py:39
  166.3 4.3 %collective-permute-start.28 = (f32[128,128]{1,0:T(8,128)S(1)}, f32[128,128]{1,0:T(8,128)S(1)}, u32[]{:S(2)}, u32[]{:S(2)}) collective-permute-start(f32[128,128]{1,0:T(8,128)S(1)} %add.343), channel_id=1, source_target_pairs={{0,24},{1,7},{2,26},{3,1},{4,28},{5,3},{6,30},{7,5},{8,0},{9,15},{... | collective-permute-start | bytes 196616 | tf_op jit(solution)/shard_map/ppermute | solution.py:39
  168.0 5.5 %collective-permute-start.27 = (f32[128,128]{1,0:T(8,128)S(1)}, f32[128,128]{1,0:T(8,128)S(1)}, u32[]{:S(2)}, u32[]{:S(2)}) collective-permute-start(f32[128,128]{1,0:T(8,128)S(1)} %add.343), channel_id=1, source_target_pairs={{0,8},{1,3},{2,10},{3,5},{4,12},{5,7},{6,14},{7,1},{8,16},{9,11},{... | collective-permute-start | bytes 196616 | tf_op jit(solution)/shard_map/ppermute | solution.py:39
  173.5 5.8 %collective-permute-start.32 = (f32[128,128]{1,0:T(8,128)S(1)}, f32[128,128]{1,0:T(8,128)S(1)}, u32[]{:S(2)}, u32[]{:S(2)}) collective-permute-start(f32[128,128]{1,0:T(8,128)S(1)} %add_add_fusion.2), channel_id=1, source_target_pairs={{0,4},{1,17},{2,6},{3,19},{4,0},{5,21},{6,2},{7,23},{8,12},{9,25},... | collective-permute-start | bytes 196616 | tf_op jit(solution)/shard_map/ppermute | solution.py:39
  174.6 5.3 %collective-permute-start.31 = (f32[128,128]{1,0:T(8,128)S(1)}, f32[128,128]{1,0:T(8,128)S(1)}, u32[]{:S(2)}, u32[]{:S(2)}) collective-permute-start(f32[128,128]{1,0:T(8,128)S(1)} %add_add_fusion.2), channel_id=1, source_target_pairs={{0,6},{1,25},{2,0},{3,27},{4,2},{5,29},{6,4},{7,31},{8,14},{9,1},{... | collective-permute-start | bytes 196616 | tf_op jit(solution)/shard_map/ppermute | solution.py:39
  175.9 5.5 %collective-permute-start.30 = (f32[128,128]{1,0:T(8,128)S(1)}, f32[128,128]{1,0:T(8,128)S(1)}, u32[]{:S(2)}, u32[]{:S(2)}) collective-permute-start(f32[128,128]{1,0:T(8,128)S(1)} %add_add_fusion.2), channel_id=1, source_target_pairs={{0,2},{1,9},{2,4},{3,11},{4,6},{5,13},{6,0},{7,15},{8,10},{9,17},{... | collective-permute-start | bytes 196616 | tf_op jit(solution)/shard_map/ppermute | solution.py:39
  176.6 8.3 %collective-permute-start.23 = (f32[32,1024]{1,0:T(8,128)S(1)}, f32[32,1024]{1,0:T(8,128)S(1)}, u32[]{:S(2)}, u32[]{:S(2)}) collective-permute-start(f32[32,1024]{1,0:T(8,128)S(1)} %get-tuple-element.19), channel_id=1, source_target_pairs={{0,32},{32,64},{64,96},{96,0},{1,33},{33,65},{65,97},{97,1},{2,34}... | collective-permute-start | bytes 393224 | tf_op jit(solution)/shard_map/ppermute | solution.py:22
  176.6 8.3 %collective-permute-start.24 = (f32[32,1024]{1,0:T(8,128)S(1)}, f32[32,1024]{1,0:T(8,128)S(1)}, u32[]{:S(2)}, u32[]{:S(2)}) collective-permute-start(f32[32,1024]{1,0:T(8,128)S(1)} %get-tuple-element.20), channel_id=1, source_target_pairs={{0,64},{32,96},{64,0},{96,32},{1,65},{33,97},{65,1},{97,33},{2,66}... | collective-permute-start | bytes 393224 | tf_op jit(solution)/shard_map/ppermute | solution.py:22
  179.4 6.7 %collective-permute-start.25 = (f32[32,1024]{1,0:T(8,128)S(1)}, f32[32,1024]{1,0:T(8,128)S(1)}, u32[]{:S(2)}, u32[]{:S(2)}) collective-permute-start(f32[32,1024]{1,0:T(8,128)S(1)} %get-tuple-element.21), channel_id=1, source_target_pairs={{0,96},{32,0},{64,32},{96,64},{1,97},{33,1},{65,33},{97,65},{2,98}... | collective-permute-start | bytes 393224 | tf_op jit(solution)/shard_map/ppermute | solution.py:22
  181.3 7.3 %collective-permute-start.35 = (f32[128,128]{1,0:T(8,128)S(1)}, f32[128,128]{1,0:T(8,128)S(1)}, u32[]{:S(2)}, u32[]{:S(2)}) collective-permute-start(f32[128,128]{1,0:T(8,128)S(1)} %add_add_fusion.1), channel_id=1, source_target_pairs={{0,64},{32,96},{64,0},{96,32},{1,65},{33,97},{65,1},{97,33},{2,66}... | collective-permute-start | bytes 196616 | tf_op jit(solution)/shard_map/ppermute | solution.py:22
  182.9 5.8 %collective-permute-start.34 = (f32[128,128]{1,0:T(8,128)S(1)}, f32[128,128]{1,0:T(8,128)S(1)}, u32[]{:S(2)}, u32[]{:S(2)}) collective-permute-start(f32[128,128]{1,0:T(8,128)S(1)} %add_add_fusion.1), channel_id=1, source_target_pairs={{0,96},{32,0},{64,32},{96,64},{1,97},{33,1},{65,33},{97,65},{2,98}... | collective-permute-start | bytes 196616 | tf_op jit(solution)/shard_map/ppermute | solution.py:22
  184.9 1.2 copy-start.8
  184.9 5.5 %collective-permute-start.33 = (f32[128,128]{1,0:T(8,128)S(1)}, f32[128,128]{1,0:T(8,128)S(1)}, u32[]{:S(2)}, u32[]{:S(2)}) collective-permute-start(f32[128,128]{1,0:T(8,128)S(1)} %add_add_fusion.1), channel_id=1, source_target_pairs={{0,32},{32,64},{64,96},{96,0},{1,33},{33,65},{65,97},{97,1},{2,34}... | collective-permute-start | bytes 196616 | tf_op jit(solution)/shard_map/ppermute | solution.py:22
  184.9 1.2 copy-start.9
  186.1 0.6 copy-start.10

commit v2 on v1

--- a/solution.py
+++ b/solution.py
@@ -9,8 +9,6 @@
 PARAMS = 128
 ITERS = 3
 NY, NX, NZ = 4, 4, 4
-PAIRS = [(i, j) for i in range(NY) for j in range(i, NY)]
-HALF = len(PAIRS) // 2
 VMEM, SMEM = pltpu.VMEM, pltpu.SMEM
 
 
@@ -55,41 +53,70 @@
     return lax.dot_general(a, b, (((ca,), (cb,)), ((), ())), preferred_element_type=F32)
 
 
-def gram_kernel(table, w0, w1, w2, w3, send, keep, hi_out, lo_out, hi, lo, sem):
-    for k, w in enumerate((w0, w1, w2, w3)):
+def product(hl, i, j, core, out):
+    half = hl.shape[2] // 2
+    send = pl.ds(pl.multiple_of((1 - core) * half, half), half)
+    keep = pl.ds(pl.multiple_of(core * half, half), half)
+    left = jnp.concatenate([hl[i, 0, send, :], hl[i, 0, keep, :], hl[i, 1, send, :], hl[i, 1, keep, :]], 0)
+    by_h, by_l = dot(left, hl[j, 0], 1, 1), dot(left, hl[j, 1], 1, 1)
+    out[0][...] = by_h[:half] + (by_h[2 * half : 3 * half] + by_l[:half] + by_l[2 * half : 3 * half])
+    out[1][...] = by_h[half : 2 * half] + (by_h[3 * half :] + by_l[half : 2 * half] + by_l[3 * half :])
+
+
+def own_kernel(table, slab, send, keep, hl_out, hl):
+    h, l = split2(slab[...])
+    hl[0, 0], hl[0, 1] = h, l
+    width = hl_out.shape[2]
+    mine = pl.ds(pl.multiple_of(table[1] * width, 128), width)
+    hl_out[0], hl_out[1] = hl[0, 0, :, mine], hl[0, 1, :, mine]
+    product(hl, 0, 0, table[0], (send, keep))
+
+
+def early_kernel(table, w1, w3, hl0, send0, keep0, send, keep, hl1, hl3, hl, sem):
+    copy = pltpu.make_async_copy(hl0, hl.at[0], sem)
+    copy.start()
+    for w, out, d in ((w1, hl3, 3), (w3, hl1, 1)):
         h, l = split2(w[...])
-        hi[table[k]] = h
-        lo[table[k]] = l
-    copies = [
-        pltpu.make_async_copy(hi, hi_out, sem.at[0]),
-        pltpu.make_async_copy(lo, lo_out, sem.at[1]),
-    ]
+        out[0], out[1] = h, l
+        hl[d, 0], hl[d, 1] = h, l
+    send[0], keep[0] = send0[...], keep0[...]
+    copy.wait()
+    for n in range(3):
+        product(hl, table[2 + 2 * n], table[3 + 2 * n], table[0], (send.at[n + 1], keep.at[n + 1]))
+
+
+def late_kernel(table, w2, hl0, hl1, hl3, send, keep, hl2, hl, sem):
+    copies = [pltpu.make_async_copy(x, hl.at[d], sem.at[d]) for x, d in ((hl0, 0), (hl3, 3), (hl1, 1))]
     for copy in copies:
         copy.start()
-    for n in range(2 * HALF):
-        i, j = table[NY + 2 * n], table[NY + 2 * n + 1]
-        out = send if n < HALF else keep
-        out[n % HALF] = dot(hi[i], hi[j], 1, 1) + (
-            (dot(hi[i], lo[j], 1, 1) + dot(lo[i], hi[j], 1, 1)) + dot(lo[i], lo[j], 1, 1)
-        )
-    for copy in copies:
-        copy.wait()
-
-
-def partial_gram(table, parts):
-    rows, cols = parts[0].shape
-    blocks = jax.ShapeDtypeStruct((HALF, rows, rows), F32)
-    halves = jax.ShapeDtypeStruct((NY, rows, cols), BF16)
+    h, l = split2(w2[...])
+    hl2[0], hl2[1] = h, l
+    hl[2, 0], hl[2, 1] = h, l
+    for n in range(3):
+        copies[n].wait()
+        product(hl, table[8 + 2 * n], table[9 + 2 * n], table[0], (send.at[n], keep.at[n]))
+
+
+def gram_call(kernel, name, table, vmem_args, any_args, more_args, blocks, wide, halves, cols):
+    rows = 256
+    struct = jax.ShapeDtypeStruct
+    vmem, anywhere = pl.BlockSpec(memory_space=VMEM), pl.BlockSpec(memory_space=pl.ANY)
+    half = struct((blocks, rows // 2, rows) if blocks else (rows // 2, rows), F32)
+    scratch = [VMEM((4 if any_args else 1, 2, rows, wide), BF16)]
+    if any_args:
+        scratch.append(pltpu.SemaphoreType.DMA((4,)) if len(any_args) > 1 else pltpu.SemaphoreType.DMA)
     return pl.pallas_call(
-        gram_kernel,
-        out_shape=(blocks, blocks, halves, halves),
-        in_specs=[pl.BlockSpec(memory_space=SMEM)] + [pl.BlockSpec(memory_space=VMEM)] * 4,
-        out_specs=[pl.BlockSpec(memory_space=VMEM)] * 2 + [pl.BlockSpec(memory_space=pl.ANY)] * 2,
-        scratch_shapes=[VMEM((NY, rows, cols), BF16)] * 2 + [pltpu.SemaphoreType.DMA((2,))],
-        compiler_params=pltpu.CompilerParams(vmem_limit_bytes=40 * 2**20),
-        cost_estimate=pl.CostEstimate(flops=2 * 40 * rows * rows * cols, bytes_accessed=11 * 2**20, transcendentals=0),
-        name="partial_gram",
-    )(table, *parts)
+        kernel,
+        out_shape=[half, half] + [struct((2, rows, cols), BF16)] * halves,
+        in_specs=[pl.BlockSpec(memory_space=SMEM)] + [vmem] * len(vmem_args) + [anywhere] * len(any_args) + [vmem] * len(more_args),
+        out_specs=[vmem] * (2 + halves),
+        scratch_shapes=scratch,
+        compiler_params=pltpu.CompilerParams(vmem_limit_bytes=24 * 2**20),
+        cost_estimate=pl.CostEstimate(
+            flops=8 * rows * rows * wide * max(blocks, 1), bytes_accessed=6 * 2**20, transcendentals=0
+        ),
+        name=name,
+    )(table, *vmem_args, *any_args, *more_args)
 
 
 def row_of(v, k):
@@ -127,39 +154,34 @@
     return jnp.concatenate(panels, 0)
 
 
-def solve_kernel(
-    place, rank, *refs, scale
-):
-    pieces, (start, hi_in, lo_in) = refs[:8], refs[8:11]
-    basis_out, core0, core1, core2, core3, param_out = refs[11:17]
-    packed, gh, gm, gl, hi, lo, work, core, sem = refs[17:]
-    copies = [
-        pltpu.make_async_copy(hi_in, hi, sem.at[0]),
-        pltpu.make_async_copy(lo_in, lo, sem.at[1]),
-    ]
+def solve_kernel(place, rank, *refs, scale):
+    pieces, start, hl_in = refs[:8], refs[8], refs[9:13]
+    basis_out, core0, core1, core2, core3, param_out = refs[13:19]
+    packed, gh, gm, gl, hl, work, core, qhl, sem = refs[19:]
+    copies = [pltpu.make_async_copy(x, hl.at[d], sem.at[d]) for d, x in enumerate(hl_in)]
     for copy in copies:
         copy.start()
-    rows = pieces[0].shape[1]
+    blocks, rows, t = pieces[0].shape
     for n, piece in enumerate(pieces):
-        for j in range(NX):
-            at = pl.multiple_of(place[NY + NX * n + j] * rows, 8)
-            packed[pl.ds(at, rows), :] = piece[j]
-    t = packed.shape[1]
-    for n, (i, j) in enumerate(PAIRS):
-        block = packed[n * t : (n + 1) * t, :] * scale
+        mine = place[12] if n < NX else 1 - place[12]
+        at = pl.multiple_of(mine * (t // 2) + place[NY + n] * rows, rows)
+        packed[:, pl.ds(at, rows), :] = piece[...]
+    for n in range(blocks):
+        i, j = place[13 + n], place[13 + blocks + n]
+        block = packed[n] * scale
         for k, g in enumerate(split3(block)):
-            (gh, gm, gl)[k][i * t : (i + 1) * t, j * t : (j + 1) * t] = g
-        if i < j:
+            (gh, gm, gl)[k][i, :, pl.ds(pl.multiple_of(j * t, t), t)] = g
+        if n < 6:
             for k, g in enumerate(split3(block.T)):
-                (gh, gm, gl)[k][j * t : (j + 1) * t, i * t : (i + 1) * t] = g
+                (gh, gm, gl)[k][j, :, pl.ds(pl.multiple_of(i * t, t), t)] = g
 
     q = start[...].T
     n = q.shape[0]
     for _ in range(ITERS):
         h, m, l = split3(q)
-        by_h = dot(jnp.concatenate([h, m, l], 0), gh[...], 1, 0)
-        by_m = dot(jnp.concatenate([h, m], 0), gm[...], 1, 0)
-        by_l = dot(h, gl[...], 1, 0)
+        by_h = dot(jnp.concatenate([h, m, l], 0), gh[...].reshape(NY * t, NY * t), 1, 0)
+        by_m = dot(jnp.concatenate([h, m], 0), gm[...].reshape(NY * t, NY * t), 1, 0)
+        by_l = dot(h, gl[...].reshape(NY * t, NY * t), 1, 0)
         image = by_h[:n] + ((by_h[n : 2 * n] + by_m[:n]) + (by_h[2 * n :] + by_m[n:] + by_l))
         h, m, l = split3(image)
         by_h = dot(jnp.concatenate([h, m, l], 0), h, 1, 1)
@@ -173,14 +195,14 @@
     slot = lax.broadcasted_iota(jnp.int32, q.shape, 0)
     q = jnp.where(slot < rank[0], q, 0.0)
     basis_out[...] = q.T
-    for copy in copies:
-        copy.wait()
-    h, l = split2(q)
+    qhl[0], qhl[1] = split2(q)
     total = None
-    for i in range(NY):
-        hs, ls = h[:, i * t : (i + 1) * t], l[:, i * t : (i + 1) * t]
-        by_hi = dot(jnp.concatenate([hs, ls], 0), hi[i], 1, 0)
-        term = by_hi[:n] + (by_hi[n:] + dot(hs, lo[i], 1, 0))
+    for d in range(NY):
+        copies[d].wait()
+        at = pl.ds(pl.multiple_of(place[d] * t, t), t)
+        hs, ls = qhl[0, :, at], qhl[1, :, at]
+        by_hi = dot(jnp.concatenate([hs, ls], 0), hl[d, 0], 1, 0)
+        term = by_hi[:n] + (by_hi[n:] + dot(hs, hl[d, 1], 1, 0))
         total = term if total is None else total + term
     core[...] = total
     own = n // NY
@@ -195,9 +217,10 @@
     param_out[...] = param
 
 
-def solve(place, rank, pieces, start_basis, hi, lo, scale):
+def solve(place, rank, pieces, start_basis, hls, scale):
     time_all, ranks = start_basis.shape
-    t, width = hi.shape[1:]
+    blocks, _, t = pieces[0].shape
+    width = hls[0].shape[2]
     struct = jax.ShapeDtypeStruct
     part = struct((ranks // NY, width), F32)
     vmem = pl.BlockSpec(memory_space=VMEM)
@@ -210,23 +233,23 @@
     return pl.pallas_call(
         body,
         out_shape=(struct((time_all, ranks), F32), part, part, part, part, struct((PARAMS, PARAMS), F32)),
-        in_specs=[smem, smem] + [vmem] * 9 + [anywhere] * 2,
+        in_specs=[smem, smem] + [vmem] * 9 + [anywhere] * 4,
         out_specs=[vmem] * 6,
         scratch_shapes=[
-            VMEM((len(PAIRS) * t, t), F32),
-            VMEM((time_all, time_all), BF16),
-            VMEM((time_all, time_all), BF16),
-            VMEM((time_all, time_all), BF16),
-            VMEM(hi.shape, BF16),
-            VMEM(lo.shape, BF16),
+            VMEM((blocks, t, t), F32),
+            VMEM((NY, t, time_all), BF16),
+            VMEM((NY, t, time_all), BF16),
+            VMEM((NY, t, time_all), BF16),
+            VMEM((NY, 2, t, width), BF16),
             VMEM((ranks, 2 * ranks), F32),
             VMEM((ranks, width), F32),
-            pltpu.SemaphoreType.DMA((2,)),
+            VMEM((2, ranks, time_all), BF16),
+            pltpu.SemaphoreType.DMA((NY,)),
         ],
-        compiler_params=pltpu.CompilerParams(vmem_limit_bytes=48 * 2**20),
+        compiler_params=pltpu.CompilerParams(vmem_limit_bytes=36 * 2**20),
         cost_estimate=pl.CostEstimate(flops=8 * 10**9, bytes_accessed=9 * 2**20, transcendentals=0),
         name="solve",
-    )(place, rank, *pieces, start_basis, hi, lo)
+    )(place, rank, *pieces, start_basis, *hls)
 
 
 def join_kernel(place, p0, p1, p2, p3, out):
@@ -246,13 +269,14 @@
     )(place, *pieces)
 
 
-def take(v, i):
-    return lax.dynamic_index_in_dim(v, i, 0, keepdims=False)
-
-
 def scatter_sum(v, me, move):
-    got = [move(take(v, (me + k) % NX), k) for k in (1, 3, 2)]
-    return take(v, me) + got[0] + got[1] + got[2]
+    v = v.reshape(v.shape[0], NX, v.shape[1] // NX, v.shape[2])
+
+    def slot(k):
+        return lax.dynamic_index_in_dim(v, (me + k) % NX, 1, keepdims=False)
+
+    got = [move(slot(k), k) for k in (1, 3, 2)]
+    return slot(0) + got[0] + got[1] + got[2]
 
 
 def exchange_sum(v, move):
@@ -278,33 +302,60 @@
     second_me = jnp.where(core_id == 0, me_z, me_x)
     four = jnp.arange(NY, dtype=jnp.int32)
 
-    def columns(k):
-        return lax.dynamic_slice_in_dim(slab, (me_y + k) % NY * width, width, 1)
-
-    got = {k: along_y(columns(k), k) for k in (1, 3, 2)}
-    parts = [columns(0), got[1], got[2], got[3]]
-    source_y = (me_y - four) % NY
-    pairs = jnp.array(PAIRS, jnp.int32).reshape(2, HALF * 2)
-    table = jnp.concatenate([source_y, take(pairs, 1 - core_id), take(pairs, core_id)])
-    send, keep, hi, lo = partial_gram(table, parts)
-
-    rows = HALF * time_local // (NX * NZ)
-    v = (keep + along_core(send)).reshape(NX, NZ, rows, time_local)
-    v = scatter_sum(v, first_me, lambda u, k: along_xz(u, k, True))
-    v = scatter_sum(v, second_me, lambda u, k: along_xz(u, k, False))
-    v = exchange_sum(v, along_y)
-    v = jnp.stack(gather(v, lambda u, k: along_xz(u, k, False)))
+    def columns(v, k):
+        return lax.dynamic_slice_in_dim(v, (me_y + k) % NY * width, width, 1)
+
+    v, got = slab, {}
+    for k in (1, 3, 2):
+        out = columns(v, k)
+        v, out = lax.optimization_barrier((v, out))
+        got[k] = along_y(out, k)
+    source_y, ahead = (me_y - four) % NY, (me_y + four) % NY
+
+    def low_first(i, j):
+        swap = ahead[i] > ahead[j]
+        return [jnp.where(swap, j, i), jnp.where(swap, i, j)]
+
+    fixed = [jnp.int32(n) for n in (0, 1, 3, 0, 2, 3, 1, 2)]
+    table = jnp.stack(
+        [core_id, me_y] + fixed[:4] + low_first(3, 1) + low_first(0, 2) + fixed[4:]
+    ).astype(jnp.int32)
+
+    def plane_sum(send, keep):
+        u = keep + along_core(send)
+        u = scatter_sum(u, first_me, lambda w, k: along_xz(w, k, True))
+        return exchange_sum(u, lambda w, k: along_xz(w, k, False))
+
+    send0, keep0, hl0 = gram_call(own_kernel, "own_gram", table, [slab], [], [], 0, columns_local, 1, width)
+    send, keep, hl1, hl3 = gram_call(
+        early_kernel, "early_gram", table, [got[1], got[3]], [hl0], [send0, keep0], 4, width, 2, width
+    )
+    early = plane_sum(send, keep)
+    early, w2 = lax.optimization_barrier((early, got[2]))
+    send, keep, hl2 = gram_call(late_kernel, "late_gram", table, [w2], [hl0, hl1, hl3], [], 3, width, 1, width)
+    late = plane_sum(send, keep)
+
+    v = jnp.concatenate([early, late])
+    got = {k: along_y(v, k) for k in (1, 3, 2)}
+    at = [v, got[3], got[2], got[1]]
+
+    def term(d, n):
+        return at[d % NY][n]
+
+    v = jnp.stack(
+        [term(d, 1) + term(d + 1, 2) + term(d + 2, 5) + term(d + 3, 6) for d in range(NY)]
+        + [term(d, 4) + term(d + 2, 4) + term(d + 1, 3) + term(d + 3, 3) for d in range(2)]
+        + [term(d, 0) for d in range(NY)]
+    )
     pieces = gather(v, lambda u, k: along_xz(u, k, True))
     pieces = pieces + [along_core(piece) for piece in pieces]
-
-    def chunk(core, first, second):
-        k, j = four[:, None], four[None, :]
-        return ((core * NX + (first - k) % NX) * NZ + (second - j) % NZ).reshape(-1)
-
+    rows_of = [ahead[d] for d in range(NY)] + [jnp.minimum(ahead[d], ahead[d + 2]) for d in range(2)]
+    cols_of = [ahead[(d + 1) % NY] for d in range(NY)] + [jnp.maximum(ahead[d], ahead[d + 2]) for d in range(2)]
     place = jnp.concatenate(
-        [(me_y + four) % NY, chunk(core_id, first_me, second_me), chunk(1 - core_id, second_me, first_me)]
-    )
-    basis, *cores, param = solve(place, time_rank, pieces, start_basis, hi, lo, 1.0 / columns_all)
+        [ahead, (first_me - four) % NX, (second_me - four) % NX]
+        + [jnp.stack([core_id] + rows_of + list(ahead) + cols_of + list(ahead))]
+    ).astype(jnp.int32)
+    basis, *cores, param = solve(place, time_rank, pieces, start_basis, [hl0, hl1, hl2, hl3], 1.0 / columns_all)
 
     param = param + along_core(param)
     param = exchange_sum(param, lambda u, k: along_xz(u, k, True))

time: 191 us -> 194 us (1.016)
  waiting for transfers between devices: 90.4 us -> 70 us
  local copies, waits for them, and re-layouts: 13.2 us -> 21.6 us
  between operations: 1.53 us -> 9.3 us
  starting transfers between devices: 42.1 us -> 46.9 us
  Pallas kernels: 40.3 us -> 44 us
    ppermute x12, waiting for transfers between devices: 52.5 us -> 33.4 us  [along_y(): return lax.ppermute(v, 'tm', [(i, (i + k) % NY) for i in range(NY)])]
    unnamed x26 -> x37, local copies, waits for them, and re-layouts: 8.89 us -> 14.1 us
    ppermute x18 -> x21, starting transfers between devices: 27.1 us -> 31.9 us  [along_xz(): return lax.ppermute(v, 'rest', perm)]
    add x5 -> x4, other arithmetic: 2.7 us -> 0.19 us  [the longest x2 0.12 us: plane_sum(): u = keep + along_core(send)]
    ppermute x6 -> x7, waiting for transfers between devices: 4.96 us -> 2.62 us  [along_core(): return lax.ppermute(v, 'rest', [(i, i ^ 1) for i in range(2 * NX * NZ)])]
    pallas_call x1 -> x3, Pallas kernels: 8.81 us -> 11.1 us  [gram_call(): pl.pallas_call(kernel, out_shape=[half, half] + [struct((2, rows, cols),...]
    dynamic_slice x1 -> x3, local copies, waits for them, and re-layouts: 3.98 us -> 5.95 us  [columns(): return lax.dynamic_slice_in_dim(v, (me_y + k) % NY * width, width, 1)]
    ppermute x18 -> x21, waiting for transfers between devices: 32.9 us -> 34 us  [along_xz(): return lax.ppermute(v, 'rest', perm)]
  transfers between devices with their start and end apart: 36 -> 40, of which waited for: 29 -> 28; matrix products, arithmetic and copies ran while one was open for 0% -> 2% of each run, Pallas kernels for 1% -> 3%
where the time goes in v2:
time: 194 us; the launch traced here: 193 us
  waiting for transfers between devices  70 us (36%)
  starting transfers between devices  46.9 us (24%)
  Pallas kernels  44 us (23%)
  local copies, waits for them, and re-layouts  21.6 us (11%)
  between operations  9.3 us (5%)
    ppermute x21, waiting for transfers between devices, along_xz(): return lax.ppermute(v, 'rest', perm)  34 us
    ppermute x12, waiting for transfers between devices, along_y(): return lax.ppermute(v, 'tm', [(i, (i + k) % NY) for i in range(NY)])  33.4 us
    ppermute x21, starting transfers between devices, along_xz(): return lax.ppermute(v, 'rest', perm)  31.9 us
    pallas_call x1, Pallas kernels, solve(): pl.pallas_call(body, out_shape=(struct((time_all, ranks), F32), part, par...  31 us
    unnamed x37, local copies, waits for them, and re-layouts  14.1 us
    ppermute x12, starting transfers between devices, along_y(): return lax.ppermute(v, 'tm', [(i, (i + k) % NY) for i in range(NY)])  14 us
    pallas_call x3, Pallas kernels, gram_call(): pl.pallas_call(kernel, out_shape=[half, half] + [struct((2, rows, cols),...  11.1 us
    dynamic_slice x3, local copies, waits for them, and re-layouts, columns(): return lax.dynamic_slice_in_dim(v, (me_y + k) % NY * width, width, 1)  5.95 us
  transfers between devices with their start and end apart: 40, of which 28 were waited for; matrix products, arithmetic and copies ran while one was open for 2% of the time, Pallas kernels for 3%

profile of v2, /device:TPU:0, one launch (start us, length us, event | category | flops | bytes accessed | tf_op | source)
XLA Modules:
  0.0 193.5 jit_solution(10143757177577993602)
XLA Ops:
  0.7 1.3 constant_dynamic-slice_fusion.2
  2.0 2.3 %constant_dynamic-slice_fusion.1 = f32[256,1024]{1,0:T(8,128)} fusion(f32[256,4096]{1,0:T(8,128)} %slab.1, s32[]{:T(128)S(6)} %select_n.138), kind=kLoop, calls=%fused_computation.47 | loop fusion | bytes 2097156 | tf_op jit(solution)/shard_map/dynamic_slice | solution.py:306
  4.3 3.1 %collective-permute-start.1 = (f32[256,1024]{1,0:T(8,128)}, f32[256,1024]{1,0:T(8,128)S(1)}, u32[]{:S(2)}, u32[]{:S(2)}) collective-permute-start(f32[256,1024]{1,0:T(8,128)} %constant_dynamic-slice_fusion.1), channel_id=1, source_target_pairs={{0,96},{32,0},{64,32},{96,64},{1,97},{33,1},{65,33},{97,65},{2,98}... | collective-permute-start | bytes 3145736 | tf_op jit(solution)/shard_map/ppermute | solution.py:20
  10.8 2.2 %copy-done = f32[256,4096]{1,0:T(8,128)S(1)} copy-done((f32[256,4096]{1,0:T(8,128)S(1)}, f32[256,4096]{1,0:T(8,128)}, u32[]{:S(2)}) %copy-start) | copy-done | bytes 4194328
  12.9 4.0 %own_gram.1 = (f32[128,256]{1,0:T(8,128)S(1)}, f32[128,256]{1,0:T(8,128)S(1)}, bf16[2,256,1024]{2,1,0:T(8,128)(2,1)S(1)}) custom-call(s32[14]{0:T(128)S(1)} %stack.10.table, f32[256,4096]{1,0:T(8,128)S(1)} %copy-done), custom_call_target="tpu_custom_call" | custom-call | flops 2147483648 | bytes 6291456 | tf_op jit(solution)/shard_map/own_gram/pallas_call | solution.py:108
  17.0 13.2 %collective-permute-done.1.w3 = f32[256,1024]{1,0:T(8,128)S(1)} collective-permute-done((f32[256,1024]{1,0:T(8,128)}, f32[256,1024]{1,0:T(8,128)S(1)}, u32[]{:S(2)}, u32[]{:S(2)}) %collective-permute-start.1) | collective-permute-done | bytes 1048608 | tf_op jit(solution)/shard_map/ppermute | solution.py:20
  30.1 3.1 %collective-permute-done.w1 = f32[256,1024]{1,0:T(8,128)S(1)} collective-permute-done((f32[256,1024]{1,0:T(8,128)S(1)}, f32[256,1024]{1,0:T(8,128)S(1)}, u32[]{:S(2)}, u32[]{:S(2)}) %collective-permute-start) | collective-permute-done | bytes 1048608 | tf_op jit(solution)/shard_map/ppermute | solution.py:20
  33.2 2.8 %early_gram.1 = (f32[4,128,256]{2,1,0:T(8,128)S(1)}, f32[4,128,256]{2,1,0:T(8,128)S(1)}, bf16[2,256,1024]{2,1,0:T(8,128)(2,1)S(1)}, bf16[2,256,1024]{2,1,0:T(8,128)(2,1)S(1)}) custom-call(s32[14]{0:T(128)S(1)} %stack.10.table, f32[256,1024]{1,0:T(8,128)S(1)} %collective-permute-done.w1, f32[256,1024]{1,0:T(8,128)S(1)} %collective-permute-done.1.w3, ...), custom_call_target="tpu_custom_call" | custom-call | flops 2147483648 | bytes 6291456 | tf_op jit(solution)/shard_map/early_gram/pallas_call | solution.py:108
  36.1 1.0 copy-done.6
  37.1 1.0 copy-done.9
  38.1 2.3 %constant_dynamic-slice_fusion = f32[256,1024]{1,0:T(8,128)} fusion(f32[256,4096]{1,0:T(8,128)} %slab.1, s32[]{:T(128)S(6)} %select_n.148), kind=kLoop, calls=%fused_computation.46 | loop fusion | bytes 2097156 | tf_op jit(solution)/shard_map/dynamic_slice | solution.py:306
  40.5 1.6 collective-permute-start.3
  42.1 1.7 collective-permute-start.4
  43.8 1.8 collective-permute-start.5
  45.6 1.1 collective-permute-done.3
  47.0 3.2 %collective-permute-done.5 = f32[4,32,256]{2,1,0:T(8,128)S(1)} collective-permute-done((f32[4,32,256]{2,1,0:T(8,128)S(1)}, f32[4,32,256]{2,1,0:T(8,128)S(1)}, u32[]{:S(2)}, u32[]{:S(2)}) %collective-permute-start.5) | collective-permute-done | bytes 131104 | tf_op jit(solution)/shard_map/ppermute | solution.py:37
  50.3 4.0 %collective-permute-start.8 = (f32[4,32,256]{2,1,0:T(8,128)S(1)}, f32[4,32,256]{2,1,0:T(8,128)S(1)}, u32[]{:S(2)}, u32[]{:S(2)}) collective-permute-start(f32[4,32,256]{2,1,0:T(8,128)S(1)} %fusion.1), channel_id=1, source_target_pairs={{0,4},{1,17},{2,6},{3,19},{4,0},{5,21},{6,2},{7,23},{8,12},{9,25},... | collective-permute-start | bytes 393224 | tf_op jit(solution)/shard_map/ppermute | solution.py:37
  54.3 0.7 collective-permute-start.7
  55.0 1.3 collective-permute-start.6
  56.3 0.9 collective-permute-done.8
  57.2 2.4 %collective-permute-done.7 = f32[4,32,256]{2,1,0:T(8,128)S(1)} collective-permute-done((f32[4,32,256]{2,1,0:T(8,128)S(1)}, f32[4,32,256]{2,1,0:T(8,128)S(1)}, u32[]{:S(2)}, u32[]{:S(2)}) %collective-permute-start.7) | collective-permute-done | bytes 131104 | tf_op jit(solution)/shard_map/ppermute | solution.py:37
  59.6 1.5 collective-permute-done.6
  61.2 6.5 %collective-permute-done.9.w2 = f32[256,1024]{1,0:T(8,128)S(1)} collective-permute-done((f32[256,1024]{1,0:T(8,128)}, f32[256,1024]{1,0:T(8,128)S(1)}, u32[]{:S(2)}, u32[]{:S(2)}) %collective-permute-start.9) | collective-permute-done | bytes 1048608 | tf_op jit(solution)/shard_map/ppermute | solution.py:20
  67.7 1.2 copy-done.4
  68.9 1.2 copy-done.7
  70.1 1.2 copy-done.10
  71.3 4.2 %late_gram.1 = (f32[3,128,256]{2,1,0:T(8,128)S(1)}, f32[3,128,256]{2,1,0:T(8,128)S(1)}, bf16[2,256,1024]{2,1,0:T(8,128)(2,1)S(1)}) custom-call(s32[14]{0:T(128)S(1)} %stack.10.table, f32[256,1024]{1,0:T(8,128)S(1)} %collective-permute-done.9.w2, bf16[2,256,1024]{2,1,0:T(8,128)(2,1)S(1)} %copy-done.4, bf16[2,256,1024]{2,1,0:T(8,128)(2,1)S(1)} %copy-done.7, ...), custom_call_target="tpu_custom_call" | custom-call | flops 1610612736 | bytes 6291456 | tf_op jit(solution)/shard_map/late_gram/pallas_call | solution.py:108
  75.7 1.7 collective-permute-done.10
  77.5 1.6 collective-permute-start.11
  79.1 1.7 collective-permute-start.12
  80.8 1.8 collective-permute-start.13
  82.6 0.8 collective-permute-done.11
  83.7 3.2 %collective-permute-done.13 = f32[3,32,256]{2,1,0:T(8,128)S(1)} collective-permute-done((f32[3,32,256]{2,1,0:T(8,128)S(1)}, f32[3,32,256]{2,1,0:T(8,128)S(1)}, u32[]{:S(2)}, u32[]{:S(2)}) %collective-permute-start.13) | collective-permute-done | bytes 98336 | tf_op jit(solution)/shard_map/ppermute | solution.py:37
  87.0 4.1 %collective-permute-start.16 = (f32[3,32,256]{2,1,0:T(8,128)S(1)}, f32[3,32,256]{2,1,0:T(8,128)S(1)}, u32[]{:S(2)}, u32[]{:S(2)}) collective-permute-start(f32[3,32,256]{2,1,0:T(8,128)S(1)} %fusion.3), channel_id=1, source_target_pairs={{0,4},{1,17},{2,6},{3,19},{4,0},{5,21},{6,2},{7,23},{8,12},{9,25},... | collective-permute-start | bytes 294920 | tf_op jit(solution)/shard_map/ppermute | solution.py:37
  91.1 0.7 collective-permute-start.15
  91.8 1.3 collective-permute-start.14
  93.7 2.1 %collective-permute-done.15 = f32[3,32,256]{2,1,0:T(8,128)S(1)} collective-permute-done((f32[3,32,256]{2,1,0:T(8,128)S(1)}, f32[3,32,256]{2,1,0:T(8,128)S(1)}, u32[]{:S(2)}, u32[]{:S(2)}) %collective-permute-start.15) | collective-permute-done | bytes 98336 | tf_op jit(solution)/shard_map/ppermute | solution.py:37
  95.8 1.9 collective-permute-done.14
  97.8 1.9 %collective-permute-start.18 = (f32[7,32,256]{2,1,0:T(8,128)S(1)}, f32[7,32,256]{2,1,0:T(8,128)S(1)}, u32[]{:S(2)}, u32[]{:S(2)}) collective-permute-start(f32[7,32,256]{2,1,0:T(8,128)S(1)} %pad_maximum_fusion), channel_id=1, source_target_pairs={{0,64},{32,96},{64,0},{96,32},{1,65},{33,97},{65,1},{97,33},{2,66}... | collective-permute-start | bytes 688136 | tf_op jit(solution)/shard_map/ppermute | solution.py:20
  99.7 1.3 collective-permute-start.17
  101.0 7.8 %collective-permute-done.19 = f32[7,32,256]{2,1,0:T(8,128)S(1)} collective-permute-done((f32[7,32,256]{2,1,0:T(8,128)S(1)}, f32[7,32,256]{2,1,0:T(8,128)S(1)}, u32[]{:S(2)}, u32[]{:S(2)}) %collective-permute-start.19) | collective-permute-done | bytes 229408 | tf_op jit(solution)/shard_map/ppermute | solution.py:20
  110.2 1.2 collective-permute-start.21
  111.9 4.9 %collective-permute-done.22.refs_5_ = f32[10,32,256]{2,1,0:T(8,128)S(1)} collective-permute-done((f32[10,32,256]{2,1,0:T(8,128)S(1)}, f32[10,32,256]{2,1,0:T(8,128)S(1)}, u32[]{:S(2)}, u32[]{:S(2)}) %collective-permute-start.22) | collective-permute-done | bytes 327712 | tf_op jit(solution)/shard_map/ppermute | solution.py:37
  117.2 1.7 collective-permute-done.21.refs_4_
  118.9 3.4 %collective-permute-done.20.refs_3_ = f32[10,32,256]{2,1,0:T(8,128)S(1)} collective-permute-done((f32[10,32,256]{2,1,0:T(8,128)S(1)}, f32[10,32,256]{2,1,0:T(8,128)S(1)}, u32[]{:S(2)}, u32[]{:S(2)}) %collective-permute-start.20) | collective-permute-done | bytes 327712 | tf_op jit(solution)/shard_map/ppermute | solution.py:37
  128.9 1.2 copy-done.5
  130.1 1.2 copy-done.8
  131.3 1.2 copy-done.11
  132.6 1.2 copy-done.13
  133.8 31.0 %solve.1 = (f32[1024,128]{1,0:T(8,128)}, f32[32,1024]{1,0:T(8,128)S(1)}, f32[32,1024]{1,0:T(8,128)S(1)}, f32[32,1024]{1,0:T(8,128)S(1)}, f32[32,1024]{1,0:T(8,128)S(1)}, /*index=5*/f32[128,128]{1,0:T(8,128)S(1)}) custom-call(s32[33]{0:T(128)S(1)} %concatenate.6.refs_0_, s32[1]{0:T(128)S(6)} %copy.31.refs_1_, ...), custom_call_target="tpu_custom_call" | custom-call | flops 8000000000 | bytes 9437184 | tf_op jit(solution)/shard_map/solve/pallas_call | solution.py:233
  165.9 0.9 collective-permute-done.30
  166.8 1.3 collective-permute-start.33
  168.2 1.2 collective-permute-start.32
  169.4 0.8 collective-permute-start.31
  170.2 2.5 %collective-permute-done.33 = f32[128,128]{1,0:T(8,128)S(1)} collective-permute-done((f32[128,128]{1,0:T(8,128)S(1)}, f32[128,128]{1,0:T(8,128)S(1)}, u32[]{:S(2)}, u32[]{:S(2)}) %collective-permute-start.33) | collective-permute-done | bytes 65568 | tf_op jit(solution)/shard_map/ppermute | solution.py:37
  172.7 2.1 %collective-permute-done.31 = f32[128,128]{1,0:T(8,128)S(1)} collective-permute-done((f32[128,128]{1,0:T(8,128)S(1)}, f32[128,128]{1,0:T(8,128)S(1)}, u32[]{:S(2)}, u32[]{:S(2)}) %collective-permute-start.31) | collective-permute-done | bytes 65568 | tf_op jit(solution)/shard_map/ppermute | solution.py:37
  174.9 1.9 collective-permute-start.36
  176.7 1.8 collective-permute-start.35
  179.0 3.6 %collective-permute-start.28 = (f32[32,1024]{1,0:T(8,128)S(1)}, f32[32,1024]{1,0:T(8,128)S(1)}, u32[]{:S(2)}, u32[]{:S(2)}) collective-permute-start(f32[32,1024]{1,0:T(8,128)S(1)} %get-tuple-element.46), channel_id=1, source_target_pairs={{0,64},{32,96},{64,0},{96,32},{1,65},{33,97},{65,1},{97,33},{2,66}... | collective-permute-start | bytes 393224 | tf_op jit(solution)/shard_map/ppermute | solution.py:20
  183.0 0.9 collective-permute-done.34
  184.0 1.1 collective-permute-start.39
  185.1 2.3 %collective-permute-start.38 = (f32[128,128]{1,0:T(8,128)S(1)}, f32[128,128]{1,0:T(8,128)S(1)}, u32[]{:S(2)}, u32[]{:S(2)}) collective-permute-start(f32[128,128]{1,0:T(8,128)S(1)} %add_add_fusion.2), channel_id=1, source_target_pairs={{0,96},{32,0},{64,32},{96,64},{1,97},{33,1},{65,33},{97,65},{2,98}... | collective-permute-start | bytes 196616 | tf_op jit(solution)/shard_map/ppermute | solution.py:20
  189.3 1.9 join_columns.1
  191.2 1.6 collective-permute-done.37
  (88 shorter events, 10.1 us)
Async XLA Ops:
  4.3 25.8 %collective-permute-start.1 = (f32[256,1024]{1,0:T(8,128)}, f32[256,1024]{1,0:T(8,128)S(1)}, u32[]{:S(2)}, u32[]{:S(2)}) collective-permute-start(f32[256,1024]{1,0:T(8,128)} %constant_dynamic-slice_fusion.1), channel_id=1, source_target_pairs={{0,96},{32,0},{64,32},{96,64},{1,97},{33,1},{65,33},{97,65},{2,98}... | collective-permute-start | bytes 3145736 | tf_op jit(solution)/shard_map/ppermute | solution.py:20
  7.4 25.8 %collective-permute-start = (f32[256,1024]{1,0:T(8,128)S(1)}, f32[256,1024]{1,0:T(8,128)S(1)}, u32[]{:S(2)}, u32[]{:S(2)}) collective-permute-start(f32[256,1024]{1,0:T(8,128)S(1)} %constant_dynamic-slice_fusion.2), channel_id=1, source_target_pairs={{0,32},{32,64},{64,96},{96,0},{1,33},{33,65},{65,97},{97,1},{2,34}... | collective-permute-start | bytes 3145736 | tf_op jit(solution)/shard_map/ppermute | solution.py:20
  10.8 2.2 %copy-start = (f32[256,4096]{1,0:T(8,128)S(1)}, f32[256,4096]{1,0:T(8,128)}, u32[]{:S(2)}) copy-start(f32[256,4096]{1,0:T(8,128)} %slab.1) | copy-start | bytes 12582916
  17.0 19.1 %copy-start.3 = (bf16[2,256,1024]{2,1,0:T(8,128)(2,1)}, bf16[2,256,1024]{2,1,0:T(8,128)(2,1)S(1)}, u32[]{:S(2)}) copy-start(bf16[2,256,1024]{2,1,0:T(8,128)(2,1)S(1)} %get-tuple-element.29.hl0.refs_11_) | copy-start | bytes 3145732
  36.1 1.0 copy-start.6
  37.1 1.0 copy-start.9
  38.1 2.3 %collective-permute-start.2 = (f32[4,128,256]{2,1,0:T(8,128)S(1)}, f32[4,128,256]{2,1,0:T(8,128)S(1)}, u32[]{:S(2)}, u32[]{:S(2)}) collective-permute-start(f32[4,128,256]{2,1,0:T(8,128)S(1)} %get-tuple-element.33), channel_id=1, source_target_pairs={{0,1},{1,0},{2,3},{3,2},{4,5},{5,4},{6,7},{7,6},{8,9},{9,8},{10,11... | collective-permute-start | bytes 1572872 | tf_op jit(solution)/shard_map/ppermute | solution.py:24
  40.4 27.3 %collective-permute-start.9 = (f32[256,1024]{1,0:T(8,128)}, f32[256,1024]{1,0:T(8,128)S(1)}, u32[]{:S(2)}, u32[]{:S(2)}) collective-permute-start(f32[256,1024]{1,0:T(8,128)} %constant_dynamic-slice_fusion), channel_id=1, source_target_pairs={{0,64},{32,96},{64,0},{96,32},{1,65},{33,97},{65,1},{97,33},{2,66}... | collective-permute-start | bytes 3145736 | tf_op jit(solution)/shard_map/ppermute | solution.py:20
  40.5 6.2 %collective-permute-start.3 = (f32[4,32,256]{2,1,0:T(8,128)S(1)}, f32[4,32,256]{2,1,0:T(8,128)S(1)}, u32[]{:S(2)}, u32[]{:S(2)}) collective-permute-start(f32[4,32,256]{2,1,0:T(8,128)S(1)} %get-tuple-element.49), channel_id=1, source_target_pairs={{0,8},{1,3},{2,10},{3,5},{4,12},{5,7},{6,14},{7,1},{8,16},{9,11},{... | collective-permute-start | bytes 393224 | tf_op jit(solution)/shard_map/ppermute | solution.py:37
  42.1 5.0 %collective-permute-start.4 = (f32[4,32,256]{2,1,0:T(8,128)S(1)}, f32[4,32,256]{2,1,0:T(8,128)S(1)}, u32[]{:S(2)}, u32[]{:S(2)}) collective-permute-start(f32[4,32,256]{2,1,0:T(8,128)S(1)} %get-tuple-element.50), channel_id=1, source_target_pairs={{0,24},{1,7},{2,26},{3,1},{4,28},{5,3},{6,30},{7,5},{8,0},{9,15},{... | collective-permute-start | bytes 393224 | tf_op jit(solution)/shard_map/ppermute | solution.py:37
  43.8 6.5 %collective-permute-start.5 = (f32[4,32,256]{2,1,0:T(8,128)S(1)}, f32[4,32,256]{2,1,0:T(8,128)S(1)}, u32[]{:S(2)}, u32[]{:S(2)}) collective-permute-start(f32[4,32,256]{2,1,0:T(8,128)S(1)} %get-tuple-element.51), channel_id=1, source_target_pairs={{0,16},{1,5},{2,18},{3,7},{4,20},{5,1},{6,22},{7,3},{8,24},{9,13},... | collective-permute-start | bytes 393224 | tf_op jit(solution)/shard_map/ppermute | solution.py:37
  50.3 6.9 %collective-permute-start.8 = (f32[4,32,256]{2,1,0:T(8,128)S(1)}, f32[4,32,256]{2,1,0:T(8,128)S(1)}, u32[]{:S(2)}, u32[]{:S(2)}) collective-permute-start(f32[4,32,256]{2,1,0:T(8,128)S(1)} %fusion.1), channel_id=1, source_target_pairs={{0,4},{1,17},{2,6},{3,19},{4,0},{5,21},{6,2},{7,23},{8,12},{9,25},... | collective-permute-start | bytes 393224 | tf_op jit(solution)/shard_map/ppermute | solution.py:37
  54.3 5.4 %collective-permute-start.7 = (f32[4,32,256]{2,1,0:T(8,128)S(1)}, f32[4,32,256]{2,1,0:T(8,128)S(1)}, u32[]{:S(2)}, u32[]{:S(2)}) collective-permute-start(f32[4,32,256]{2,1,0:T(8,128)S(1)} %fusion.1), channel_id=1, source_target_pairs={{0,6},{1,25},{2,0},{3,27},{4,2},{5,29},{6,4},{7,31},{8,14},{9,1},{... | collective-permute-start | bytes 393224 | tf_op jit(solution)/shard_map/ppermute | solution.py:37
  55.0 6.2 %collective-permute-start.6 = (f32[4,32,256]{2,1,0:T(8,128)S(1)}, f32[4,32,256]{2,1,0:T(8,128)S(1)}, u32[]{:S(2)}, u32[]{:S(2)}) collective-permute-start(f32[4,32,256]{2,1,0:T(8,128)S(1)} %fusion.1), channel_id=1, source_target_pairs={{0,2},{1,9},{2,4},{3,11},{4,6},{5,13},{6,0},{7,15},{8,10},{9,17},{... | collective-permute-start | bytes 393224 | tf_op jit(solution)/shard_map/ppermute | solution.py:37
  67.7 1.2 copy-start.4
  68.9 1.2 copy-start.7
  70.1 1.2 copy-start.10
  71.3 57.5 %copy-start.2 = (f32[1024,128]{1,0:T(8,128)S(1)}, f32[1024,128]{1,0:T(8,128)}, u32[]{:S(2)}) copy-start(f32[1024,128]{1,0:T(8,128)} %refs_10_.1) | copy-start | bytes 1572868
  75.6 46.8 %copy-start.12 = (bf16[2,256,1024]{2,1,0:T(8,128)(2,1)}, bf16[2,256,1024]{2,1,0:T(8,128)(2,1)S(1)}, u32[]{:S(2)}) copy-start(bf16[2,256,1024]{2,1,0:T(8,128)(2,1)S(1)} %get-tuple-element.42.refs_13_) | copy-start | bytes 3145732
  75.6 1.8 collective-permute-start.10
  77.5 5.9 %collective-permute-start.11 = (f32[3,32,256]{2,1,0:T(8,128)S(1)}, f32[3,32,256]{2,1,0:T(8,128)S(1)}, u32[]{:S(2)}, u32[]{:S(2)}) collective-permute-start(f32[3,32,256]{2,1,0:T(8,128)S(1)} %get-tuple-element.52), channel_id=1, source_target_pairs={{0,8},{1,3},{2,10},{3,5},{4,12},{5,7},{6,14},{7,1},{8,16},{9,11},{... | collective-permute-start | bytes 294920 | tf_op jit(solution)/shard_map/ppermute | solution.py:37
  79.1 4.6 %collective-permute-start.12 = (f32[3,32,256]{2,1,0:T(8,128)S(1)}, f32[3,32,256]{2,1,0:T(8,128)S(1)}, u32[]{:S(2)}, u32[]{:S(2)}) collective-permute-start(f32[3,32,256]{2,1,0:T(8,128)S(1)} %get-tuple-element.53), channel_id=1, source_target_pairs={{0,24},{1,7},{2,26},{3,1},{4,28},{5,3},{6,30},{7,5},{8,0},{9,15},{... | collective-permute-start | bytes 294920 | tf_op jit(solution)/shard_map/ppermute | solution.py:37
  80.8 6.1 %collective-permute-start.13 = (f32[3,32,256]{2,1,0:T(8,128)S(1)}, f32[3,32,256]{2,1,0:T(8,128)S(1)}, u32[]{:S(2)}, u32[]{:S(2)}) collective-permute-start(f32[3,32,256]{2,1,0:T(8,128)S(1)} %get-tuple-element.54), channel_id=1, source_target_pairs={{0,16},{1,5},{2,18},{3,7},{4,20},{5,1},{6,22},{7,3},{8,24},{9,13},... | collective-permute-start | bytes 294920 | tf_op jit(solution)/shard_map/ppermute | solution.py:37
  87.0 6.7 %collective-permute-start.16 = (f32[3,32,256]{2,1,0:T(8,128)S(1)}, f32[3,32,256]{2,1,0:T(8,128)S(1)}, u32[]{:S(2)}, u32[]{:S(2)}) collective-permute-start(f32[3,32,256]{2,1,0:T(8,128)S(1)} %fusion.3), channel_id=1, source_target_pairs={{0,4},{1,17},{2,6},{3,19},{4,0},{5,21},{6,2},{7,23},{8,12},{9,25},... | collective-permute-start | bytes 294920 | tf_op jit(solution)/shard_map/ppermute | solution.py:37
  91.1 4.7 %collective-permute-start.15 = (f32[3,32,256]{2,1,0:T(8,128)S(1)}, f32[3,32,256]{2,1,0:T(8,128)S(1)}, u32[]{:S(2)}, u32[]{:S(2)}) collective-permute-start(f32[3,32,256]{2,1,0:T(8,128)S(1)} %fusion.3), channel_id=1, source_target_pairs={{0,6},{1,25},{2,0},{3,27},{4,2},{5,29},{6,4},{7,31},{8,14},{9,1},{... | collective-permute-start | bytes 294920 | tf_op jit(solution)/shard_map/ppermute | solution.py:37
  91.8 5.8 %collective-permute-start.14 = (f32[3,32,256]{2,1,0:T(8,128)S(1)}, f32[3,32,256]{2,1,0:T(8,128)S(1)}, u32[]{:S(2)}, u32[]{:S(2)}) collective-permute-start(f32[3,32,256]{2,1,0:T(8,128)S(1)} %fusion.3), channel_id=1, source_target_pairs={{0,2},{1,9},{2,4},{3,11},{4,6},{5,13},{6,0},{7,15},{8,10},{9,17},{... | collective-permute-start | bytes 294920 | tf_op jit(solution)/shard_map/ppermute | solution.py:37
  97.7 11.2 %collective-permute-start.19 = (f32[7,32,256]{2,1,0:T(8,128)S(1)}, f32[7,32,256]{2,1,0:T(8,128)S(1)}, u32[]{:S(2)}, u32[]{:S(2)}) collective-permute-start(f32[7,32,256]{2,1,0:T(8,128)S(1)} %pad_maximum_fusion), channel_id=1, source_target_pairs={{0,32},{32,64},{64,96},{96,0},{1,33},{33,65},{65,97},{97,1},{2,34}... | collective-permute-start | bytes 688136 | tf_op jit(solution)/shard_map/ppermute | solution.py:20
  97.8 11.1 %collective-permute-start.18 = (f32[7,32,256]{2,1,0:T(8,128)S(1)}, f32[7,32,256]{2,1,0:T(8,128)S(1)}, u32[]{:S(2)}, u32[]{:S(2)}) collective-permute-start(f32[7,32,256]{2,1,0:T(8,128)S(1)} %pad_maximum_fusion), channel_id=1, source_target_pairs={{0,64},{32,96},{64,0},{96,32},{1,65},{33,97},{65,1},{97,33},{2,66}... | collective-permute-start | bytes 688136 | tf_op jit(solution)/shard_map/ppermute | solution.py:20
  99.7 9.8 %collective-permute-start.17 = (f32[7,32,256]{2,1,0:T(8,128)S(1)}, f32[7,32,256]{2,1,0:T(8,128)S(1)}, u32[]{:S(2)}, u32[]{:S(2)}) collective-permute-start(f32[7,32,256]{2,1,0:T(8,128)S(1)} %pad_maximum_fusion), channel_id=1, source_target_pairs={{0,96},{32,0},{64,32},{96,64},{1,97},{33,1},{65,33},{97,65},{2,98}... | collective-permute-start | bytes 688136 | tf_op jit(solution)/shard_map/ppermute | solution.py:20
  109.7 7.1 %collective-permute-start.22 = (f32[10,32,256]{2,1,0:T(8,128)S(1)}, f32[10,32,256]{2,1,0:T(8,128)S(1)}, u32[]{:S(2)}, u32[]{:S(2)}) collective-permute-start(f32[10,32,256]{2,1,0:T(8,128)S(1)} %slice_dynamic-update-slice_fusion.refs_2_), channel_id=1, source_target_pairs={{0,24},{1,7},{2,26},{3,1},{4,28},{5,3},{6,30},{7,5},{8,0},{9,15},{... | collective-permute-start | bytes 983048 | tf_op jit(solution)/shard_map/ppermute | solution.py:37
  110.2 8.7 %collective-permute-start.21 = (f32[10,32,256]{2,1,0:T(8,128)S(1)}, f32[10,32,256]{2,1,0:T(8,128)S(1)}, u32[]{:S(2)}, u32[]{:S(2)}) collective-permute-start(f32[10,32,256]{2,1,0:T(8,128)S(1)} %slice_dynamic-update-slice_fusion.refs_2_), channel_id=1, source_target_pairs={{0,16},{1,5},{2,18},{3,7},{4,20},{5,1},{6,22},{7,3},{8,24},{9,13},... | collective-permute-start | bytes 983048 | tf_op jit(solution)/shard_map/ppermute | solution.py:37
  111.5 10.9 %collective-permute-start.20 = (f32[10,32,256]{2,1,0:T(8,128)S(1)}, f32[10,32,256]{2,1,0:T(8,128)S(1)}, u32[]{:S(2)}, u32[]{:S(2)}) collective-permute-start(f32[10,32,256]{2,1,0:T(8,128)S(1)} %slice_dynamic-update-slice_fusion.refs_2_), channel_id=1, source_target_pairs={{0,8},{1,3},{2,10},{3,5},{4,12},{5,7},{6,14},{7,1},{8,16},{9,11},{... | collective-permute-start | bytes 983048 | tf_op jit(solution)/shard_map/ppermute | solution.py:37
  111.9 16.9 %collective-permute-start.23 = (f32[10,32,256]{2,1,0:T(8,128)S(1)}, f32[10,32,256]{2,1,0:T(8,128)S(1)}, u32[]{:S(2)}, u32[]{:S(2)}) collective-permute-start(f32[10,32,256]{2,1,0:T(8,128)S(1)} %slice_dynamic-update-slice_fusion.refs_2_), channel_id=1, source_target_pairs={{0,1},{1,0},{2,3},{3,2},{4,5},{5,4},{6,7},{7,6},{8,9},{9,8},{10,11... | collective-permute-start | bytes 983048 | tf_op jit(solution)/shard_map/ppermute | solution.py:24
  116.8 12.0 %collective-permute-start.26 = (f32[10,32,256]{2,1,0:T(8,128)S(1)}, f32[10,32,256]{2,1,0:T(8,128)S(1)}, u32[]{:S(2)}, u32[]{:S(2)}) collective-permute-start(f32[10,32,256]{2,1,0:T(8,128)S(1)} %collective-permute-done.22.refs_5_), channel_id=1, source_target_pairs={{0,1},{1,0},{2,3},{3,2},{4,5},{5,4},{6,7},{7,6},{8,9},{9,8},{10,11... | collective-permute-start | bytes 983048 | tf_op jit(solution)/shard_map/ppermute | solution.py:24
  118.9 9.9 %collective-permute-start.25 = (f32[10,32,256]{2,1,0:T(8,128)S(1)}, f32[10,32,256]{2,1,0:T(8,128)S(1)}, u32[]{:S(2)}, u32[]{:S(2)}) collective-permute-start(f32[10,32,256]{2,1,0:T(8,128)S(1)} %collective-permute-done.21.refs_4_), channel_id=1, source_target_pairs={{0,1},{1,0},{2,3},{3,2},{4,5},{5,4},{6,7},{7,6},{8,9},{9,8},{10,11... | collective-permute-start | bytes 983048 | tf_op jit(solution)/shard_map/ppermute | solution.py:24
  122.3 6.5 %collective-permute-start.24 = (f32[10,32,256]{2,1,0:T(8,128)S(1)}, f32[10,32,256]{2,1,0:T(8,128)S(1)}, u32[]{:S(2)}, u32[]{:S(2)}) collective-permute-start(f32[10,32,256]{2,1,0:T(8,128)S(1)} %collective-permute-done.20.refs_3_), channel_id=1, source_target_pairs={{0,1},{1,0},{2,3},{3,2},{4,5},{5,4},{6,7},{7,6},{8,9},{9,8},{10,11... | collective-permute-start | bytes 983048 | tf_op jit(solution)/shard_map/ppermute | solution.py:24
  128.9 1.2 copy-start.5
  130.1 1.2 copy-start.8
  131.3 1.2 copy-start.11
  132.6 1.2 copy-start.13
  164.8 0.7 copy-start.1
  165.4 1.4 collective-permute-start.30
  166.8 5.8 %collective-permute-start.33 = (f32[128,128]{1,0:T(8,128)S(1)}, f32[128,128]{1,0:T(8,128)S(1)}, u32[]{:S(2)}, u32[]{:S(2)}) collective-permute-start(f32[128,128]{1,0:T(8,128)S(1)} %add.310), channel_id=1, source_target_pairs={{0,16},{1,5},{2,18},{3,7},{4,20},{5,1},{6,22},{7,3},{8,24},{9,13},... | collective-permute-start | bytes 196616 | tf_op jit(solution)/shard_map/ppermute | solution.py:37
  168.2 4.5 %collective-permute-start.32 = (f32[128,128]{1,0:T(8,128)S(1)}, f32[128,128]{1,0:T(8,128)S(1)}, u32[]{:S(2)}, u32[]{:S(2)}) collective-permute-start(f32[128,128]{1,0:T(8,128)S(1)} %add.310), channel_id=1, source_target_pairs={{0,24},{1,7},{2,26},{3,1},{4,28},{5,3},{6,30},{7,5},{8,0},{9,15},{... | collective-permute-start | bytes 196616 | tf_op jit(solution)/shard_map/ppermute | solution.py:37
  169.4 5.5 %collective-permute-start.31 = (f32[128,128]{1,0:T(8,128)S(1)}, f32[128,128]{1,0:T(8,128)S(1)}, u32[]{:S(2)}, u32[]{:S(2)}) collective-permute-start(f32[128,128]{1,0:T(8,128)S(1)} %add.310), channel_id=1, source_target_pairs={{0,8},{1,3},{2,10},{3,5},{4,12},{5,7},{6,14},{7,1},{8,16},{9,11},{... | collective-permute-start | bytes 196616 | tf_op jit(solution)/shard_map/ppermute | solution.py:37
  174.9 7.7 %collective-permute-start.36 = (f32[128,128]{1,0:T(8,128)S(1)}, f32[128,128]{1,0:T(8,128)S(1)}, u32[]{:S(2)}, u32[]{:S(2)}) collective-permute-start(f32[128,128]{1,0:T(8,128)S(1)} %add_add_fusion.3), channel_id=1, source_target_pairs={{0,4},{1,17},{2,6},{3,19},{4,0},{5,21},{6,2},{7,23},{8,12},{9,25},... | collective-permute-start | bytes 196616 | tf_op jit(solution)/shard_map/ppermute | solution.py:37
  176.7 6.3 %collective-permute-start.35 = (f32[128,128]{1,0:T(8,128)S(1)}, f32[128,128]{1,0:T(8,128)S(1)}, u32[]{:S(2)}, u32[]{:S(2)}) collective-permute-start(f32[128,128]{1,0:T(8,128)S(1)} %add_add_fusion.3), channel_id=1, source_target_pairs={{0,6},{1,25},{2,0},{3,27},{4,2},{5,29},{6,4},{7,31},{8,14},{9,1},{... | collective-permute-start | bytes 196616 | tf_op jit(solution)/shard_map/ppermute | solution.py:37
  178.5 5.5 %collective-permute-start.34 = (f32[128,128]{1,0:T(8,128)S(1)}, f32[128,128]{1,0:T(8,128)S(1)}, u32[]{:S(2)}, u32[]{:S(2)}) collective-permute-start(f32[128,128]{1,0:T(8,128)S(1)} %add_add_fusion.3), channel_id=1, source_target_pairs={{0,2},{1,9},{2,4},{3,11},{4,6},{5,13},{6,0},{7,15},{8,10},{9,17},{... | collective-permute-start | bytes 196616 | tf_op jit(solution)/shard_map/ppermute | solution.py:37
  178.8 8.6 %collective-permute-start.27 = (f32[32,1024]{1,0:T(8,128)S(1)}, f32[32,1024]{1,0:T(8,128)S(1)}, u32[]{:S(2)}, u32[]{:S(2)}) collective-permute-start(f32[32,1024]{1,0:T(8,128)S(1)} %get-tuple-element.45), channel_id=1, source_target_pairs={{0,32},{32,64},{64,96},{96,0},{1,33},{33,65},{65,97},{97,1},{2,34}... | collective-permute-start | bytes 393224 | tf_op jit(solution)/shard_map/ppermute | solution.py:20
  179.0 9.3 %collective-permute-start.28 = (f32[32,1024]{1,0:T(8,128)S(1)}, f32[32,1024]{1,0:T(8,128)S(1)}, u32[]{:S(2)}, u32[]{:S(2)}) collective-permute-start(f32[32,1024]{1,0:T(8,128)S(1)} %get-tuple-element.46), channel_id=1, source_target_pairs={{0,64},{32,96},{64,0},{96,32},{1,65},{33,97},{65,1},{97,33},{2,66}... | collective-permute-start | bytes 393224 | tf_op jit(solution)/shard_map/ppermute | solution.py:20
  182.5 6.1 %collective-permute-start.29 = (f32[32,1024]{1,0:T(8,128)S(1)}, f32[32,1024]{1,0:T(8,128)S(1)}, u32[]{:S(2)}, u32[]{:S(2)}) collective-permute-start(f32[32,1024]{1,0:T(8,128)S(1)} %get-tuple-element.47), channel_id=1, source_target_pairs={{0,96},{32,0},{64,32},{96,64},{1,97},{33,1},{65,33},{97,65},{2,98}... | collective-permute-start | bytes 393224 | tf_op jit(solution)/shard_map/ppermute | solution.py:20
  184.0 7.2 %collective-permute-start.39 = (f32[128,128]{1,0:T(8,128)S(1)}, f32[128,128]{1,0:T(8,128)S(1)}, u32[]{:S(2)}, u32[]{:S(2)}) collective-permute-start(f32[128,128]{1,0:T(8,128)S(1)} %add_add_fusion.2), channel_id=1, source_target_pairs={{0,64},{32,96},{64,0},{96,32},{1,65},{33,97},{65,1},{97,33},{2,66}... | collective-permute-start | bytes 196616 | tf_op jit(solution)/shard_map/ppermute | solution.py:20
  185.1 6.2 %collective-permute-start.38 = (f32[128,128]{1,0:T(8,128)S(1)}, f32[128,128]{1,0:T(8,128)S(1)}, u32[]{:S(2)}, u32[]{:S(2)}) collective-permute-start(f32[128,128]{1,0:T(8,128)S(1)} %add_add_fusion.2), channel_id=1, source_target_pairs={{0,96},{32,0},{64,32},{96,64},{1,97},{33,1},{65,33},{97,65},{2,98}... | collective-permute-start | bytes 196616 | tf_op jit(solution)/shard_map/ppermute | solution.py:20
  187.4 1.3 copy-start.14
  187.4 5.5 %collective-permute-start.37 = (f32[128,128]{1,0:T(8,128)S(1)}, f32[128,128]{1,0:T(8,128)S(1)}, u32[]{:S(2)}, u32[]{:S(2)}) collective-permute-start(f32[128,128]{1,0:T(8,128)S(1)} %add_add_fusion.2), channel_id=1, source_target_pairs={{0,32},{32,64},{64,96},{96,0},{1,33},{33,65},{65,97},{97,1},{2,34}... | collective-permute-start | bytes 196616 | tf_op jit(solution)/shard_map/ppermute | solution.py:20
  188.3 0.7 copy-start.15
  188.6 0.7 copy-start.16
